TPU v7x, 128 devices: a whole 4x4x4 slice. The times are simulated.
128 devices in a mesh: team: 8 (over y_lo, z), rep: 16 (over x, y_hi, core).
Axes of the slice: x: 4, y: 4 (y_hi: 2, y_lo: 2; y = y_hi * 2 + y_lo), z: 4, core: 2. Of those that a mesh axis runs over, the one named last changes fastest.
Arguments:
- affinity: bfloat16 [8, 256, 8, 128, 128], P('team', 'rep'), as said below
- col_index: int32 [8, 256, 8], P('team', 'rep'), may hold values from 0 to 31, all different within a row
- labels: int32 [32768], P(('rep', 'team')), may hold values from 0 to 511
Outputs:
- diffused: bfloat16 [32768, 512], P(('rep', 'team'))
Inputs may be any that keep to these rules, and one draw needn't show every extreme that they name: `affinity`: every entry is positive. `col_index`: the 8 block columns of one block row are different.
All inputs are finite; a program needn't handle non-finite values.
Results may differ from a plain program's by a relative error of at most 0.017.
Values may be sent and summed in bfloat16 or wider, within the bound.
A program may use at most 128 MiB of HBM per device.

v0:
```python
import jax
import jax.numpy as jnp
from jax import lax
from jax.sharding import PartitionSpec as P

C = 512
ITERS = 3


def on_device(affinity, col_index, labels):
    panels = affinity[0]
    columns = col_index[0]
    block = panels.shape[-1]
    slots = panels.shape[1]
    rows_here = labels.shape[0]
    classes = jnp.arange(C, dtype=jnp.int32)
    seeded = (labels[:, None] == classes[None, :]).astype(jnp.float32) * 16.0
    current = seeded.astype(jnp.bfloat16)
    for step_index in range(ITERS):
        gathered = lax.all_gather(current, "rep", axis=0, tiled=True).reshape(-1, block, C)
        block_count = lax.axis_size("team") * rows_here // block
        summed = jnp.zeros((block_count, block, C), jnp.float32)
        for slot_index in range(slots):
            picked = gathered[columns[:, slot_index]]
            summed = summed + jnp.einsum(
                "iab,ibc->iac", panels[:, slot_index], picked, preferred_element_type=jnp.float32
            )
        summed_all = lax.psum_scatter(
            summed.reshape(lax.axis_size("team") * rows_here, C).astype(jnp.bfloat16),
            "team",
            scatter_dimension=0,
            tiled=True,
        ).astype(jnp.float32)
        blended = 0.9 * summed_all + 0.1 * seeded
        scale_rows = lax.rsqrt(jnp.mean(blended * blended, axis=-1, keepdims=True) + 1e-06)
        current = (blended * scale_rows).astype(jnp.bfloat16)
    return current


def solution(mesh):
    in_specs = (P("team", "rep", None, None, None), P("team", "rep", None), P(("rep", "team")))
    out_specs = P(("rep", "team"), None)
    return jax.shard_map(
        on_device, mesh=mesh, in_specs=in_specs, out_specs=out_specs, check_vma=False
    )
```

profile of v0, /device:TPU:0, one launch (start us, length us, event | category | flops | bytes accessed | tf_op | source)
XLA Modules:
  0.0 504.4 jit_solution(15811978290454994971)
XLA Ops:
  8.1 4.7 copy.6
  12.9 55.3 %all-gather.4.cloned.1.call-done = bf16[4096,512]{1,0:T(8,128)(2,1)} async-done(((bf16[256,512]{1,0:T(8,128)(2,1)}), bf16[4096,512]{1,0:T(8,128)(2,1)}) %all-gather.4.cloned.1.call-update) | async-done | bytes 4194320 | tf_op jit(solution)/shard_map/all_gather | solution.py:20
  68.2 2.9 gather_fusion.7
  71.1 4.2 gather_fusion.6
  75.3 4.2 gather_fusion.5
  79.5 4.2 gather_fusion.4
  83.7 4.3 gather_fusion.3
  87.9 4.2 gather_fusion.2
  92.1 4.2 gather_fusion.1
  96.3 4.2 gather_fusion
  119.2 10.8 %add_convert_fusion.2 = bf16[16,512,128]{1,2,0:T(8,128)(2,1)} fusion(f32[16,512,128]{1,2,0:T(8,128)S(1)} %fusion.21, f32[16,512,128]{1,2,0:T(8,128)S(1)} %fusion.18, f32[16,512,128]{1,2,0:T(8,128)} %fusion.15, f32[16,512,128]{1,2,0:T(8,128)} %fusion.12, f32[16,512,128]{1,2,0:T(8,128)} %fusion.9, f32[16,512,128]{1,2,0:T(8,128)} %fusion.3, ...), kind=kOutput, calls=%fused_computation.27 | convolution fusion | flops 276824064 | bytes 34078720 | tf_op jit(solution)/shard_map/iab,ibc->iac/dot_general | solution.py:25
  130.1 41.6 %reduce-scatter.4.cloned.1.call-done = bf16[256,512]{1,0:T(8,128)(2,1)} async-done(((bf16[2048,512]{1,0:T(8,128)(2,1)}), bf16[256,512]{1,0:T(8,128)(2,1)}) %reduce-scatter.4.cloned.1.call-update) | async-done | bytes 262160 | tf_op jit(solution)/shard_map/reduce_scatter | solution.py:28
  175.1 54.6 %all-gather.6.cloned.1.call-done = bf16[4096,512]{1,0:T(8,128)(2,1)} async-done(((bf16[256,512]{1,0:T(8,128)(2,1)}), bf16[4096,512]{1,0:T(8,128)(2,1)}) %all-gather.6.cloned.1.call-update) | async-done | bytes 4194320 | tf_op jit(solution)/shard_map/all_gather | solution.py:20
  232.6 4.2 gather_fusion.14
  236.8 4.3 gather_fusion.13
  241.0 4.2 gather_fusion.12
  245.2 4.2 gather_fusion.11
  249.4 4.2 gather_fusion.10
  253.6 4.2 gather_fusion.9
  257.8 4.2 gather_fusion.8
  280.7 10.8 %add_convert_fusion.1 = bf16[16,512,128]{1,2,0:T(8,128)(2,1)} fusion(f32[16,512,128]{1,2,0:T(8,128)S(1)} %fusion.22, f32[16,512,128]{1,2,0:T(8,128)S(1)} %fusion.19, f32[16,512,128]{1,2,0:T(8,128)} %fusion.16, f32[16,512,128]{1,2,0:T(8,128)} %fusion.13, f32[16,512,128]{1,2,0:T(8,128)} %fusion.10, f32[16,512,128]{1,2,0:T(8,128)} %fusion.4, ...), kind=kOutput, calls=%fused_computation.26 | convolution fusion | flops 276824064 | bytes 34078720 | tf_op jit(solution)/shard_map/iab,ibc->iac/dot_general | solution.py:25
  291.6 41.8 %reduce-scatter.6.cloned.1.call-done = bf16[256,512]{1,0:T(8,128)(2,1)} async-done(((bf16[2048,512]{1,0:T(8,128)(2,1)}), bf16[256,512]{1,0:T(8,128)(2,1)}) %reduce-scatter.6.cloned.1.call-update) | async-done | bytes 262160 | tf_op jit(solution)/shard_map/reduce_scatter | solution.py:28
  336.7 54.3 %all-gather.8.cloned.1.call-done = bf16[4096,512]{1,0:T(8,128)(2,1)} async-done(((bf16[256,512]{1,0:T(8,128)(2,1)}), bf16[4096,512]{1,0:T(8,128)(2,1)}) %all-gather.8.cloned.1.call-update) | async-done | bytes 4194320 | tf_op jit(solution)/shard_map/all_gather | solution.py:20
  393.9 4.2 gather_fusion.22
  398.1 4.2 gather_fusion.21
  402.3 4.2 gather_fusion.20
  406.5 4.3 gather_fusion.19
  410.7 4.2 gather_fusion.18
  415.0 4.2 gather_fusion.17
  419.1 4.2 gather_fusion.16
  441.9 10.7 %add_convert_fusion = bf16[16,512,128]{1,2,0:T(8,128)(2,1)} fusion(f32[16,512,128]{1,2,0:T(8,128)} %fusion.23, f32[16,512,128]{1,2,0:T(8,128)} %fusion.20, f32[16,512,128]{1,2,0:T(8,128)} %fusion.17, f32[16,512,128]{1,2,0:T(8,128)} %fusion.14, f32[16,512,128]{1,2,0:T(8,128)} %fusion.11, f32[16,512,128]{1,2,0:T(8,128)S(1)} %fusion.5, ...), kind=kOutput, calls=%fused_computation.25 | convolution fusion | flops 276824064 | bytes 34078720 | tf_op jit(solution)/shard_map/iab,ibc->iac/dot_general | solution.py:25
  452.6 41.8 %reduce-scatter.8.cloned.1.call-done = bf16[256,512]{1,0:T(8,128)(2,1)} async-done(((bf16[2048,512]{1,0:T(8,128)(2,1)}), bf16[256,512]{1,0:T(8,128)(2,1)}) %reduce-scatter.8.cloned.1.call-update) | async-done | bytes 262160 | tf_op jit(solution)/shard_map/reduce_scatter | solution.py:28
  (96 shorter events, 73.1 us)
Async XLA Ops:
  6.5 61.7 %all-gather.4.cloned.1.call-start = ((), (), s32[]{:S(2)}) async-start(), calls=%async_computation.3 | async-start | bytes 4456448 | tf_op jit(solution)/shard_map/all_gather | solution.py:20
  8.1 4.8 copy-start.22
  8.1 163.6 %reduce-scatter.4.cloned.1.call-start = ((), (), s32[]{:S(2)}) async-start(), calls=%async_computation.4 | async-start | bytes 2359296 | tf_op jit(solution)/shard_map/reduce_scatter | solution.py:28
  100.5 3.0 copy-start
  100.5 3.7 copy-start.12
  104.2 1.6 copy-start.13
  105.8 2.7 copy-start.10
  108.5 2.7 copy-start.11
  111.2 2.6 copy-start.8
  113.8 2.6 copy-start.9
  130.0 41.7 %copy-start.21 = (s32[256]{0:T(256)S(1)}, s32[256]{0:T(256)}, u32[]{:S(2)}) copy-start(s32[256]{0:T(256)} %param.5) | copy-start | bytes 3076
  130.0 99.7 %all-gather.6.cloned.1.call-start = ((), (), s32[]{:S(2)}) async-start(), calls=%async_computation.5 | async-start | bytes 4456448 | tf_op jit(solution)/shard_map/all_gather | solution.py:20
  174.8 158.5 %reduce-scatter.6.cloned.1.call-start = ((), (), s32[]{:S(2)}) async-start(), calls=%async_computation.6 | async-start | bytes 2359296 | tf_op jit(solution)/shard_map/reduce_scatter | solution.py:28
  262.0 3.0 copy-start.1
  262.0 3.7 copy-start.19
  265.7 1.6 copy-start.18
  267.2 2.7 copy-start.16
  270.0 2.7 copy-start.14
  272.7 2.6 copy-start.15
  275.3 2.6 copy-start.6
  291.5 99.5 %all-gather.8.cloned.1.call-start = ((), (), s32[]{:S(2)}) async-start(), calls=%async_computation.7 | async-start | bytes 4456448 | tf_op jit(solution)/shard_map/all_gather | solution.py:20
  336.5 158.0 %reduce-scatter.8.cloned.1.call-start = ((), (), s32[]{:S(2)}) async-start(), calls=%async_computation.8 | async-start | bytes 2359296 | tf_op jit(solution)/shard_map/reduce_scatter | solution.py:28
  423.3 3.0 copy-start.2
  423.4 3.7 copy-start.20
  427.0 1.6 copy-start.17
  428.6 2.6 copy-start.7
  431.2 2.7 copy-start.5
  434.0 2.7 copy-start.4
  436.7 2.6 copy-start.3
Sparse Core Ops, SparseCore 0:
  9.8 58.4 all-gather.3
  130.2 41.5 reduce-scatter.3
  175.0 54.6 all-gather.5
  291.6 41.6 reduce-scatter.5
  336.6 54.4 all-gather.7
  452.8 41.6 reduce-scatter.7
where the time goes:
time: 506 us; the launch traced here: 504 us
  waiting for transfers between devices  290 us (57%)
  local copies, waits for them, and re-layouts  108 us (21%)
  matrix products  82.3 us (16%)
  between operations  13.6 us (3%)
  other arithmetic  10.8 us (2%)
    all_gather x3, waiting for transfers between devices, on_device(): lax.all_gather(current, 'rep', axis=0, tiled=True).reshape(-1, block, C)  164 us
    reduce_scatter x3, waiting for transfers between devices, on_device(): lax.psum_scatter(summed.reshape(lax.axis_size('team') * rows_here, C).ast...  125 us
    gather x24, local copies, waits for them, and re-layouts, on_device(): picked = gathered[columns[:, slot_index]]  96.9 us
    dot_general x24, matrix products, on_device(): jnp.einsum('iab,ibc->iac', panels[:, slot_index], picked, preferred_eleme...  82.3 us
    unnamed x47, local copies, waits for them, and re-layouts  10.7 us
  transfers between devices with their start and end apart: 6, of which 6 were waited for; matrix products, arithmetic and copies ran while one was open for 1% of the time, Pallas kernels for 0%

commit v1 on v0

v1 whole, which is shorter than its diff:
```python
import functools

import jax
import jax.numpy as jnp
from jax import lax
from jax.experimental import pallas as pl
from jax.experimental.pallas import tpu as pltpu
from jax.sharding import PartitionSpec as P

C = 512
BLK = 128
KB = 8
ITERS = 3
ROWS = 256
N_REP = 16
MESH = pl.DeviceIdType.MESH
F32 = jnp.float32
BF16 = jnp.bfloat16

CHUNKS = ((0, 64), (64, 64), (128, 64), (192, 64))
NQ = len(CHUNKS)

DZ2, DIR, COMB = 0, 1, 2
PARTNER, LEFT, RIGHT, LEFT_P, RIGHT_P, FAR, FAR_P, OWN = range(8)


def kernel(
    aff_hbm, col, lab, out,
    aff, lab_all, x0, x1, x2, p0, p1, p2, zin, yin, zout, yout,
    aff_sem, lab_send, lab_recv, z_send, z_recv, y_send, y_recv, g_send, g_recv, s_send, s_recv,
):
    r, t = lax.axis_index("rep"), lax.axis_index("team")
    x, yh, c = r // 4, (r // 2) % 2, r % 2
    yl, z = t // 4, t % 4

    def rep_of(dx=0, dyh=0, dc=0):
        return lax.rem(x + dx + 4, 4) * 4 + lax.rem(yh + dyh, 2) * 2 + lax.rem(c + dc, 2)

    def team_of(dz=0, dyl=0):
        return lax.rem(yl + dyl, 2) * 4 + lax.rem(z + dz + 4, 4)

    def z_of(dz):
        return lax.rem(z + dz + 4, 4)

    def remote(src, dst, send, recv, rep=None, team=None):
        return pltpu.make_async_remote_copy(
            src_ref=src, dst_ref=dst, send_sem=send, recv_sem=recv,
            device_id={"team": t if team is None else team, "rep": r if rep is None else rep},
            device_id_type=MESH,
        )

    xs, ps = (x0, x1, x2), (p0, p1, p2)
    started = []

    def go(copy):
        copy.start()
        started.append(copy)

    fetch = pltpu.make_async_copy(aff_hbm, aff, aff_sem)
    fetch.start()

    barrier = pltpu.get_barrier_semaphore()
    others = [lax.rem(r + k, N_REP) for k in range(1, N_REP)]
    for other in others:
        pl.semaphore_signal(barrier, inc=1, device_id={"team": t, "rep": other}, device_id_type=MESH)
    for other in (team_of(dz=1), team_of(dz=-1), team_of(dyl=1)):
        pl.semaphore_signal(barrier, inc=1, device_id={"team": other, "rep": r}, device_id_type=MESH)
    pl.semaphore_wait(barrier, N_REP - 1 + 3)

    lab_copies = []
    for k in range(1, N_REP):
        lab_copies.append(
            remote(lab, lab_all.at[r], lab_send.at[k - 1], lab_recv.at[k - 1], rep=lax.rem(r + k, N_REP))
        )
        lab_copies[-1].start()
    channel = lax.broadcasted_iota(jnp.int32, (BLK, C), 1)

    def seed(rep, rows_of):
        for h in range(2):
            x0[2 * rep + h] = jnp.where(rows_of(h)[:, None] == channel, 16.0, 0.0).astype(BF16)

    seed(r, lambda h: lab[h])
    for k in range(1, N_REP):
        lab_copies[k - 1].wait()
    def seed_one(k, carry):
        rep = lax.rem(r + k, N_REP)
        seed(rep, lambda h: lab_all[rep, h])
        return carry
    lax.fori_loop(1, N_REP, seed_one, 0)
    fetch.wait()

    for it in range(ITERS):
        cur, p = xs[it], ps[it]
        nxt = xs[it + 1] if it + 1 < ITERS else None

        def block_row(team, h, cur=cur, p=p):
            i = 2 * team + h
            acc = None
            for s in range(0, KB, 2):
                lhs = jnp.concatenate([aff[i, s], aff[i, s + 1]], axis=1)
                rhs = jnp.concatenate([cur[col[i, s]], cur[col[i, s + 1]]], axis=0)
                d = jnp.dot(lhs, rhs, preferred_element_type=F32)
                acc = d if acc is None else acc + d
            p[team, h * BLK : (h + 1) * BLK] = acc.astype(BF16)

        def pair(dz, h):
            block_row(z_of(dz), h)
            block_row(4 + z_of(dz), h)

        def products_far(h):
            pair(2, h)

        def products_near(h):
            def body(j, carry):
                pair(1 - j, h)
                return carry
            lax.fori_loop(0, 3, body, 0)

        def rows(q):
            return pl.ds(CHUNKS[q][0], CHUNKS[q][1])

        def z_copy(kind, v, q, dz, src, it=it):
            k = 2 * kind + v
            return remote(
                src, zin.at[it, k, rows(q)], z_send.at[it, q, k], z_recv.at[it, q, k], team=team_of(dz=dz)
            )

        def ahead(v):
            return 1 if v == 0 else -1

        def far(q):
            for v in range(2):
                go(z_copy(DZ2, v, q, ahead(v), p.at[4 * v + z_of(2), rows(q)]))

        def near(q):
            for v in range(2):
                go(z_copy(DIR, v, q, -ahead(v), p.at[4 * v + z_of(-ahead(v)), rows(q)]))

        def combine(q):
            for v in range(2):
                z_copy(DZ2, v, q, ahead(v), p.at[4 * v + z_of(2), rows(q)]).wait_recv()
                total = p[4 * v + z_of(ahead(v)), rows(q)].astype(F32) + zin[it, 2 * DZ2 + v, rows(q)].astype(F32)
                zout[it, v, rows(q)] = total.astype(BF16)
                go(z_copy(COMB, v, q, ahead(v), zout.at[it, v, rows(q)]))

        def z_sum(v, q):
            return (
                p[4 * v + z, rows(q)].astype(F32)
                + zin[it, 2 * DIR + v, rows(q)].astype(F32)
                + zin[it, 2 * COMB + v, rows(q)].astype(F32)
            )

        def y_copy(q):
            return remote(yout.at[it, rows(q)], yin.at[it, rows(q)], y_send.at[it, q], y_recv.at[it, q], team=team_of(dyl=1))

        def across(q):
            for v in range(2):
                z_copy(DIR, v, q, -ahead(v), p.at[0, rows(q)]).wait_recv()
                z_copy(COMB, v, q, ahead(v), zout.at[it, v, rows(q)]).wait_recv()
            yout[it, rows(q)] = z_sum(1 - yl, q).astype(BF16)
            go(y_copy(q))

        def place(rep, q):
            first, size = CHUNKS[q]
            return 2 * rep + first // BLK, pl.ds(first % BLK, size)

        def g_copy(kind, q, to, of):
            at = nxt.at[place(of, q)]
            return remote(at, at, g_send.at[it, q, kind], g_recv.at[it, q, kind], rep=to)

        def s_copy(kind, q, of):
            at = nxt.at[place(of, q)]
            return remote(at, at, s_send.at[it, q, kind], s_recv.at[it, q, kind], rep=rep_of(dc=1))

        left, right = rep_of(dx=-1), rep_of(dx=1)
        source = {
            OWN: r,
            PARTNER: rep_of(dyh=1),
            LEFT: left,
            RIGHT: right,
            LEFT_P: rep_of(dx=-1, dyh=1),
            RIGHT_P: rep_of(dx=1, dyh=1),
            FAR: rep_of(dx=2),
            FAR_P: rep_of(dx=2, dyh=1),
        }

        def got(kind, q):
            g_copy(kind, q, r, source[kind]).wait_recv()

        def share(kind, q):
            go(s_copy(kind, q, source[kind]))

        def finish(q):
            y_copy(q).wait_recv()
            seeded = x0[place(r, q)].astype(F32)
            blended = 0.9 * (z_sum(yl, q) + yin[it, rows(q)].astype(F32)) + 0.1 * seeded
            scale = lax.rsqrt(jnp.mean(blended * blended, axis=-1, keepdims=True) + 1e-6)
            scores = (blended * scale).astype(BF16)
            if nxt is None:
                out[rows(q)] = scores
                return
            nxt[place(r, q)] = scores
            go(g_copy(PARTNER, q, rep_of(dyh=1), r))
            go(g_copy(LEFT, q, right, r))
            go(g_copy(RIGHT, q, left, r))
            share(OWN, q)

        def spread_partner(q):
            got(PARTNER, q)
            go(g_copy(LEFT_P, q, right, source[PARTNER]))
            go(g_copy(RIGHT_P, q, left, source[PARTNER]))
            share(PARTNER, q)

        def spread_own(q):
            got(LEFT, q)
            go(g_copy(FAR, q, right, source[LEFT]))
            share(LEFT, q)
            got(RIGHT, q)
            share(RIGHT, q)

        def spread_last(q):
            got(RIGHT_P, q)
            go(g_copy(FAR_P, q, left, source[RIGHT_P]))
            share(RIGHT_P, q)
            got(LEFT_P, q)
            share(LEFT_P, q)

        def spread_far(q):
            for kind in (FAR, FAR_P):
                got(kind, q)
                share(kind, q)

        products_far(0)
        far(0)
        products_near(0)
        near(0)
        far(1)
        products_far(1)
        products_near(1)
        for k in range(1, NQ + 8):
            def do(step, q):
                if 0 <= q < NQ:
                    step(q)
            do(combine, k - 1)
            do(near, k)
            do(far, k + 1)
            do(across, k - 2)
            do(finish, k - 3)
            if nxt is not None:
                do(spread_partner, k - 4)
                do(spread_own, k - 4)
                do(spread_last, k - 5)
                do(spread_far, k - 6)
        if nxt is not None:
            for q in range(NQ):
                for kind in range(8):
                    g = {OWN: rep_of(dc=1)}.get(kind)
                    s_copy(kind, q, r).wait_recv()

    for copy in started:
        copy.wait_send()


def on_device(affinity, col_index, labels):
    vmem = pl.BlockSpec(memory_space=pltpu.VMEM)
    dma = pltpu.SemaphoreType.DMA
    scores = pltpu.VMEM((2 * N_REP, BLK, C), BF16)
    partials = pltpu.VMEM((8, ROWS, C), BF16)
    return pl.pallas_call(
        kernel,
        out_shape=jax.ShapeDtypeStruct((ROWS, C), BF16),
        in_specs=[pl.BlockSpec(memory_space=pl.ANY), pl.BlockSpec(memory_space=pltpu.SMEM), vmem],
        out_specs=vmem,
        scratch_shapes=[
            pltpu.VMEM((16, KB, BLK, BLK), BF16),
            pltpu.VMEM((N_REP, 2, BLK), jnp.int32),
            scores, scores, scores,
            partials, partials, partials,
            pltpu.VMEM((ITERS, 6, ROWS, C), BF16),
            pltpu.VMEM((ITERS, ROWS, C), BF16),
            pltpu.VMEM((ITERS, 2, ROWS, C), BF16),
            pltpu.VMEM((ITERS, ROWS, C), BF16),
            dma,
            dma((N_REP - 1,)), dma((N_REP - 1,)),
            dma((ITERS, NQ, 6)), dma((ITERS, NQ, 6)),
            dma((ITERS, NQ)), dma((ITERS, NQ)),
            dma((ITERS - 1, NQ, 7)), dma((ITERS - 1, NQ, 7)),
            dma((ITERS - 1, NQ, 8)), dma((ITERS - 1, NQ, 8)),
        ],
        compiler_params=pltpu.CompilerParams(
            collective_id=0, has_side_effects=True, vmem_limit_bytes=48 * 2**20
        ),
    )(affinity[0], col_index[0], labels.reshape(2, BLK))


def solution(mesh):
    in_specs = (P("team", "rep", None, None, None), P("team", "rep", None), P(("rep", "team")))
    out_specs = P(("rep", "team"), None)
    return jax.shard_map(
        on_device, mesh=mesh, in_specs=in_specs, out_specs=out_specs, check_vma=False
    )
```

time: 506 us -> 122 us (0.24)
  waiting for transfers between devices: 290 us -> 0 us
  Pallas kernels: 0 us -> 117 us
  local copies, waits for them, and re-layouts: 108 us -> 4.33 us
  matrix products: 82.3 us -> 0 us
  between operations: 13.6 us -> 0.01 us
  other arithmetic: 10.8 us -> 0 us
    all_gather x3 -> x0, waiting for transfers between devices: 164 us -> none  [on_device(): lax.all_gather(current, 'rep', axis=0, tiled=True).reshape(-1, block, C)]
    reduce_scatter x3 -> x0, waiting for transfers between devices: 125 us -> none  [on_device(): lax.psum_scatter(summed.reshape(lax.axis_size('team') * rows_here, C).ast...]
    pallas_call x0 -> x1, Pallas kernels: none -> 117 us  [on_device(): pl.pallas_call(kernel, out_shape=jax.ShapeDtypeStruct((ROWS, C), BF16), i...]
    gather x24 -> x0, local copies, waits for them, and re-layouts: 96.9 us -> none  [on_device(): picked = gathered[columns[:, slot_index]]]
    dot_general x24 -> x0, matrix products: 82.3 us -> none  [on_device(): jnp.einsum('iab,ibc->iac', panels[:, slot_index], picked, preferred_eleme...]
    unnamed x47 -> x5, local copies, waits for them, and re-layouts: 10.7 us -> 3.57 us
    convert_element_type x4 -> x0, other arithmetic: 7.05 us -> none  [the longest x3 5.56 us: on_device(): current = (blended * scale_rows).astype(jnp.bfloat16)]
  transfers between devices with their start and end apart: 6 -> 0, of which waited for: 6 -> 0; matrix products, arithmetic and copies ran while one was open for 1% -> 0% of each run, Pallas kernels for 0% -> 0%
where the time goes in v1:
time: 122 us; the launch traced here: 121 us
  Pallas kernels  117 us (96%)
  local copies, waits for them, and re-layouts  4.33 us (4%)
    pallas_call x1, Pallas kernels, on_device(): pl.pallas_call(kernel, out_shape=jax.ShapeDtypeStruct((ROWS, C), BF16), i...  117 us
    unnamed x5, local copies, waits for them, and re-layouts  3.57 us

profile of v1, /device:TPU:0, one launch (start us, length us, event | category | flops | bytes accessed | tf_op | source)
XLA Modules:
  0.0 121.1 jit_solution(2773725333659192139)
XLA Ops:
  0.0 0.8 copy.4.col
  0.8 0.0 copy-start
  0.8 2.2 %copy-done = bf16[1,16,8,128,128]{4,3,2,1,0:T(8,128)(2,1)S(1)} copy-done((bf16[1,16,8,128,128]{4,3,2,1,0:T(8,128)(2,1)S(1)}, bf16[1,16,8,128,128]{4,3,2,1,0:T(8,128)(2,1)}, u32[]{:S(2)}) %copy-start) | copy-done | bytes 4194328
  2.9 0.0 copy-start.1
  2.9 0.7 copy-done.1
  3.6 116.8 %shard_map.37 = bf16[256,512]{1,0:T(8,128)(2,1)S(1)} custom-call(bf16[16,8,128,128]{3,2,1,0:T(8,128)(2,1)S(1)} %bitcast.3, s32[16,8]{1,0:T(8,128)S(1)} %copy.4.col, s32[2,128]{1,0:T(2,128)S(1)} %bitcast.4), custom_call_target="tpu_custom_call" | custom-call | tf_op jit(solution)/shard_map/pallas_call | solution.py:269
  120.4 0.7 copy.6
Async XLA Ops:
  0.8 2.2 %copy-start = (bf16[1,16,8,128,128]{4,3,2,1,0:T(8,128)(2,1)S(1)}, bf16[1,16,8,128,128]{4,3,2,1,0:T(8,128)(2,1)}, u32[]{:S(2)}) copy-start(bf16[1,16,8,128,128]{4,3,2,1,0:T(8,128)(2,1)} %param.3) | copy-start | bytes 12582916
  2.9 0.7 copy-start.1

commit v2 on v1

v2 whole, which is shorter than its diff:
```python
import functools

import jax
import jax.numpy as jnp
from jax import lax
from jax.experimental import pallas as pl
from jax.experimental.pallas import tpu as pltpu
from jax.sharding import PartitionSpec as P

C = 512
BLK = 128
KB = 8
ITERS = 3
ROWS = 256
N_REP = 16
MESH = pl.DeviceIdType.MESH
F32 = jnp.float32
BF16 = jnp.bfloat16

CHUNKS = (
    (0, 32, "Z", "P"),
    (32, 32, "Z", "P"),
    (64, 64, "Y", "X"),
    (128, 64, "Z", "P"),
    (192, 32, "Z", "P"),
    (224, 32, "Z", "D"),
)
ORDER = (
    ("m", 0), ("F", 0), ("m", 1), ("F", 1), ("F", 3), ("n", 0), ("o", 0), ("Y", 2), ("N", 0), ("C", 0), ("n", 1),
    ("N", 1), ("F", 4), ("C", 1), ("o", 1), ("N", 3), ("C", 3), ("A", 0), ("C", 4), ("A", 1), ("F", 5), ("E", 0),
    ("N", 4), ("W", 2), ("A", 3), ("C", 5), ("E", 1), ("N", 5), ("A", 4), ("L", 0), ("P", 0), ("C", 2), ("E", 3),
    ("A", 5), ("R", 0), ("P", 1), ("E", 4), ("E", 2), ("E", 5), ("R", 1), ("R", 2), ("P", 3), ("L", 2), ("L", 5),
    ("P", 2), ("P", 4), ("L", 1), ("M", 0), ("P", 5), ("L", 3), ("K", 1), ("M", 1), ("G", 2), ("R", 3), ("M", 3),
    ("L", 4), ("G", 5), ("K", 5), ("M", 4), ("R", 5), ("K", 0), ("R", 4), ("M", 5), ("G", 0), ("K", 3), ("H", 1),
    ("K", 4), ("M", 2), ("G", 1), ("H", 0), ("K", 2), ("H", 5), ("G", 3), ("H", 2), ("G", 4), ("H", 3), ("H", 4),
)
CHUNKS_LAST = (
    (0, 64, "Z", "P"),
    (64, 64, "Z", "P"),
    (128, 64, "Z", "P"),
    (192, 64, "Y", "P"),
)
ORDER_LAST = (
    ("m", 0), ("F", 0), ("n", 0), ("F", 1), ("m", 1), ("N", 1), ("n", 1), ("o", 1), ("F", 2), ("C", 0), ("Y", 3),
    ("C", 1), ("o", 0), ("N", 0), ("C", 2), ("N", 2), ("A", 1), ("W", 3), ("A", 0), ("A", 2), ("C", 3), ("E", 1),
    ("E", 0), ("E", 2), ("E", 3),
)
NQ = max(len(CHUNKS), len(CHUNKS_LAST))

DZ2, DIR, COMB = 0, 1, 2
PARTNER, LEFT, RIGHT, LEFT_P, RIGHT_P, FAR, FAR_P, OWN, FAR_2 = range(9)


def kernel(
    aff_hbm, col, lab, out,
    aff, lab_all, x0, x1, x2, p0, p1, p2, zin, yin, zout, yout, yall, ysum,
    aff_sem, lab_send, lab_recv, z_send, z_recv, y_send, y_recv, g_send, g_recv, s_send, s_recv,
):
    r, t = lax.axis_index("rep"), lax.axis_index("team")
    x, yh, c = r // 4, (r // 2) % 2, r % 2
    yl, z = t // 4, t % 4

    def rep_of(dx=0, dyh=0, dc=0):
        return lax.rem(x + dx + 4, 4) * 4 + lax.rem(yh + dyh, 2) * 2 + lax.rem(c + dc, 2)

    def team_of(dz=0, dyl=0):
        return lax.rem(yl + dyl, 2) * 4 + lax.rem(z + dz + 4, 4)

    def z_of(dz):
        return lax.rem(z + dz + 4, 4)

    def remote(src, dst, send, recv, rep=None, team=None):
        return pltpu.make_async_remote_copy(
            src_ref=src, dst_ref=dst, send_sem=send, recv_sem=recv,
            device_id={"team": t if team is None else team, "rep": r if rep is None else rep},
            device_id_type=MESH,
        )

    xs, ps = (x0, x1, x2), (p0, p1, p2)
    started = []

    def go(copy):
        copy.start()
        started.append(copy)

    fetch = pltpu.make_async_copy(aff_hbm, aff, aff_sem)
    fetch.start()

    barrier = pltpu.get_barrier_semaphore()
    others = [lax.rem(r + k, N_REP) for k in range(1, N_REP)]
    for other in others:
        pl.semaphore_signal(barrier, inc=1, device_id={"team": t, "rep": other}, device_id_type=MESH)
    for other in (team_of(dz=1), team_of(dz=-1), team_of(dyl=1)):
        pl.semaphore_signal(barrier, inc=1, device_id={"team": other, "rep": r}, device_id_type=MESH)
    pl.semaphore_wait(barrier, N_REP - 1 + 3)

    lab_copies = []
    for k in range(1, N_REP):
        lab_copies.append(
            remote(lab, lab_all.at[r], lab_send.at[k - 1], lab_recv.at[k - 1], rep=lax.rem(r + k, N_REP))
        )
        lab_copies[-1].start()
    channel = lax.broadcasted_iota(jnp.int32, (BLK, C), 1)

    def seed(rep, rows_of):
        for h in range(2):
            x0[2 * rep + h] = jnp.where(rows_of(h)[:, None] == channel, 16.0, 0.0).astype(BF16)

    seed(r, lambda h: lab[h])
    for k in range(1, N_REP):
        lab_copies[k - 1].wait()
    def seed_one(k, carry):
        rep = lax.rem(r + k, N_REP)
        seed(rep, lambda h: lab_all[rep, h])
        return carry
    lax.fori_loop(1, N_REP, seed_one, 0, unroll=3)
    fetch.wait()

    for it in range(ITERS):
        cur, p = xs[it], ps[it]
        nxt = xs[it + 1] if it + 1 < ITERS else None
        chunks, order = (CHUNKS, ORDER) if nxt is not None else (CHUNKS_LAST, ORDER_LAST)

        def block_row(team, h, cur=cur, p=p):
            i = 2 * team + h
            acc = None
            for s in range(0, KB, 2):
                lhs = jnp.concatenate([aff[i, s], aff[i, s + 1]], axis=1)
                rhs = jnp.concatenate([cur[col[s, i]], cur[col[s + 1, i]]], axis=0)
                d = jnp.dot(lhs, rhs, preferred_element_type=F32)
                acc = d if acc is None else acc + d
            p[team, h * BLK : (h + 1) * BLK] = acc.astype(BF16)

        def pair(dz, h):
            block_row(z_of(dz), h)
            block_row(4 + z_of(dz), h)

        def products_far(h):
            pair(2, h)

        def products_near(h):
            def body(j, carry):
                pair(1 - 2 * j, h)
                return carry
            lax.fori_loop(0, 2, body, 0)

        def products_here(h):
            pair(0, h)

        def rows(q):
            return pl.ds(chunks[q][0], chunks[q][1])

        def part(v, q):
            first, size, way, _ = chunks[q]
            return pl.ds(first, size) if way == "Z" else pl.ds(first + v * (size // 2), size // 2)

        def ahead(v):
            return 1 if v == 0 else -1

        def z_copy(kind, v, q, src):
            k = 2 * kind + v
            dz = -ahead(v) if kind == DIR else ahead(v)
            return remote(
                src, zin.at[it, k, part(v, q)], z_send.at[it, q, k], z_recv.at[it, q, k], team=team_of(dz=dz)
            )

        def term(v, dz, q):
            if chunks[q][2] == "Z":
                return p.at[4 * v + z_of(dz), part(v, q)]
            return ysum.at[it, z_of(dz), part(v, q)]

        def z_got(kind, v, q):
            z_copy(kind, v, q, zout.at[it, v, part(v, q)]).wait_recv()

        def far(q):
            for v in range(2):
                go(z_copy(DZ2, v, q, term(v, 2, q)))

        def near(q):
            for v in range(2):
                go(z_copy(DIR, v, q, term(v, -ahead(v), q)))

        def combine(q):
            for v in range(2):
                z_got(DZ2, v, q)
                total = term(v, ahead(v), q)[...].astype(F32) + zin[it, 2 * DZ2 + v, part(v, q)].astype(F32)
                zout[it, v, part(v, q)] = total.astype(BF16)
                go(z_copy(COMB, v, q, zout.at[it, v, part(v, q)]))

        def z_sum(v, q):
            return (
                term(v, 0, q)[...].astype(F32)
                + zin[it, 2 * DIR + v, part(v, q)].astype(F32)
                + zin[it, 2 * COMB + v, part(v, q)].astype(F32)
            )

        def y_copy(q):
            return remote(yout.at[it, rows(q)], yin.at[it, rows(q)], y_send.at[it, q], y_recv.at[it, q], team=team_of(dyl=1))

        def y_all_copy(q):
            return remote(
                p.at[pl.ds(4 * (1 - yl), 4), rows(q)], yall.at[it, :, rows(q)],
                y_send.at[it, q], y_recv.at[it, q], team=team_of(dyl=1),
            )

        def z_arrived(q):
            for v in range(2):
                z_got(DIR, v, q)
                z_got(COMB, v, q)

        def across(q):
            z_arrived(q)
            yout[it, rows(q)] = z_sum(1 - yl, q).astype(BF16)
            go(y_copy(q))

        def across_first(q):
            go(y_all_copy(q))

        def around(q):
            y_all_copy(q).wait_recv()
            for k in range(4):
                total = p[4 * yl + k, rows(q)].astype(F32) + yall[it, k, rows(q)].astype(F32)
                ysum[it, k, rows(q)] = total.astype(BF16)
            far(q)
            near(q)

        def place(rep, q, half=None):
            first, size = chunks[q][:2]
            if half is not None:
                first, size = first + half * (size // 2), size // 2
            return 2 * rep + first // BLK, pl.ds(first % BLK, size)

        left, right, partner = rep_of(dx=-1), rep_of(dx=1), rep_of(dyh=1)
        source = {
            OWN: r,
            PARTNER: partner,
            LEFT: left,
            RIGHT: right,
            LEFT_P: rep_of(dx=-1, dyh=1),
            RIGHT_P: rep_of(dx=1, dyh=1),
            FAR: rep_of(dx=2),
            FAR_P: rep_of(dx=2, dyh=1),
        }

        def g_copy(kind, q, to, of, half=None):
            at = nxt.at[place(of, q, half)]
            sem = FAR_2 if half == 1 else kind
            return remote(at, at, g_send.at[it, q, sem], g_recv.at[it, q, sem], rep=to)

        def s_copy(kind, q, of):
            at = nxt.at[place(of, q)]
            return remote(at, at, s_send.at[it, q, kind], s_recv.at[it, q, kind], rep=rep_of(dc=1))

        def finish(q):
            if chunks[q][2] == "Z":
                y_copy(q).wait_recv()
                sums = z_sum(yl, q) + yin[it, rows(q)].astype(F32)
            else:
                z_arrived(q)
                sums = jnp.concatenate([z_sum(0, q), z_sum(1, q)], axis=0)
            seeded = x0[place(r, q)].astype(F32)
            blended = 0.9 * sums + 0.1 * seeded
            scale = lax.rsqrt(jnp.mean(blended * blended, axis=-1, keepdims=True) + 1e-6)
            scores = (blended * scale).astype(BF16)
            if nxt is None:
                out[rows(q)] = scores
                return
            nxt[place(r, q)] = scores
            go(g_copy(PARTNER, q, partner, r))
            go(g_copy(LEFT, q, right, r))
            go(g_copy(RIGHT, q, left, r))
            if chunks[q][3] == "D":
                go(g_copy(LEFT_P, q, rep_of(dx=1, dyh=1), r))
                go(g_copy(RIGHT_P, q, rep_of(dx=-1, dyh=1), r))
                go(g_copy(FAR, q, rep_of(dx=2), r))
                go(g_copy(FAR_P, q, rep_of(dx=2, dyh=1), r))
            go(s_copy(OWN, q, r))

        def spread(kind, q):
            of, way = source[kind], chunks[q][3]
            halved = way == "X" and kind == FAR
            g_copy(kind, q, r, of, 0 if halved else None).wait_recv()
            if halved:
                g_copy(kind, q, r, of, 1).wait_recv()
            if way == "P":
                if kind == PARTNER:
                    go(g_copy(LEFT_P, q, right, of))
                    go(g_copy(RIGHT_P, q, left, of))
                if kind == LEFT:
                    go(g_copy(FAR, q, right, of))
                if kind == RIGHT_P:
                    go(g_copy(FAR_P, q, left, of))
            if way == "X":
                if kind == LEFT:
                    go(g_copy(FAR, q, right, of, 0))
                    go(g_copy(LEFT_P, q, partner, of))
                if kind == RIGHT:
                    go(g_copy(FAR, q, left, of, 1))
                    go(g_copy(RIGHT_P, q, partner, of))
                if kind == FAR:
                    go(g_copy(FAR_P, q, partner, of))
            go(s_copy(kind, q, of))

        steps = dict(
            m=products_far, n=products_near, o=products_here, F=far, N=near, C=combine, A=across,
            Y=across_first, W=around, E=finish,
            P=functools.partial(spread, PARTNER), L=functools.partial(spread, LEFT), R=functools.partial(spread, RIGHT),
            K=functools.partial(spread, LEFT_P), M=functools.partial(spread, RIGHT_P),
            G=functools.partial(spread, FAR), H=functools.partial(spread, FAR_P),
        )
        for step, q in order:
            steps[step](q)
        if nxt is not None:
            for q in range(len(chunks)):
                for kind in range(8):
                    s_copy(kind, q, r).wait_recv()

    for copy in started:
        copy.wait_send()


def on_device(affinity, col_index, labels):
    vmem = pl.BlockSpec(memory_space=pltpu.VMEM)
    dma = pltpu.SemaphoreType.DMA
    scores = pltpu.VMEM((2 * N_REP, BLK, C), BF16)
    partials = pltpu.VMEM((8, ROWS, C), BF16)
    return pl.pallas_call(
        kernel,
        out_shape=jax.ShapeDtypeStruct((ROWS, C), BF16),
        in_specs=[pl.BlockSpec(memory_space=pl.ANY), pl.BlockSpec(memory_space=pltpu.SMEM), vmem],
        out_specs=vmem,
        scratch_shapes=[
            pltpu.VMEM((16, KB, BLK, BLK), BF16),
            pltpu.VMEM((N_REP, 2, BLK), jnp.int32),
            scores, scores, scores,
            partials, partials, partials,
            pltpu.VMEM((ITERS, 6, ROWS, C), BF16),
            pltpu.VMEM((ITERS, ROWS, C), BF16),
            pltpu.VMEM((ITERS, 2, ROWS, C), BF16),
            pltpu.VMEM((ITERS, ROWS, C), BF16),
            pltpu.VMEM((ITERS, 4, ROWS, C), BF16),
            pltpu.VMEM((ITERS, 4, ROWS, C), BF16),
            dma,
            dma((N_REP - 1,)), dma((N_REP - 1,)),
            dma((ITERS, NQ, 6)), dma((ITERS, NQ, 6)),
            dma((ITERS, NQ)), dma((ITERS, NQ)),
            dma((ITERS - 1, NQ, 9)), dma((ITERS - 1, NQ, 9)),
            dma((ITERS - 1, NQ, 8)), dma((ITERS - 1, NQ, 8)),
        ],
        compiler_params=pltpu.CompilerParams(
            collective_id=0, has_side_effects=True, vmem_limit_bytes=60 * 2**20
        ),
    )(affinity[0], col_index[0].T, labels.reshape(2, BLK))


def solution(mesh):
    in_specs = (P("team", "rep", None, None, None), P("team", "rep", None), P(("rep", "team")))
    out_specs = P(("rep", "team"), None)
    return jax.shard_map(
        on_device, mesh=mesh, in_specs=in_specs, out_specs=out_specs, check_vma=False
    )
```

time: 122 us -> 112 us (0.918)
  Pallas kernels: 117 us -> 109 us
  local copies, waits for them, and re-layouts: 4.33 us -> 1.67 us
    pallas_call x1, Pallas kernels: 117 us -> 109 us  [on_device(): pl.pallas_call(kernel, out_shape=jax.ShapeDtypeStruct((ROWS, C), BF16), i...]
    unnamed x5 -> x1, local copies, waits for them, and re-layouts: 3.57 us -> 1.67 us
where the time goes in v2:
time: 112 us; the launch traced here: 110 us
  Pallas kernels  109 us (97%)
  local copies, waits for them, and re-layouts  1.67 us (1%)
    pallas_call x1, Pallas kernels, on_device(): pl.pallas_call(kernel, out_shape=jax.ShapeDtypeStruct((ROWS, C), BF16), i...  109 us

profile of v2, /device:TPU:0, one launch (start us, length us, event | category | flops | bytes accessed | tf_op | source)
XLA Modules:
  0.0 110.3 jit_solution(15649625601697165071)
XLA Ops:
  0.0 108.6 %shard_map.37 = bf16[256,512]{1,0:T(8,128)(2,1)} custom-call(bf16[16,8,128,128]{3,2,1,0:T(8,128)(2,1)} %bitcast.5, s32[8,16]{1,0:T(8,128)} %bitcast.6, s32[2,128]{1,0:T(2,128)} %bitcast.7), custom_call_target="tpu_custom_call" | custom-call | tf_op jit(solution)/shard_map/pallas_call | solution.py:327
  108.7 1.7 %copy.5 = bf16[256,512]{1,0:T(8,128)(2,1)} copy(bf16[256,512]{1,0:T(8,128)(2,1)} %shard_map.37) | data formatting | bytes 524288

commit v3 on v0

v3 whole, which is shorter than its diff:
```python
import functools

import jax
import jax.numpy as jnp
from jax import lax
from jax.experimental import pallas as pl
from jax.experimental.pallas import tpu as pltpu
from jax.sharding import PartitionSpec as P

C = 512
BLK = 128
KB = 8
ITERS = 3
ROWS = 256
N_REP = 16
MESH = pl.DeviceIdType.MESH
F32 = jnp.float32
BF16 = jnp.bfloat16

CHUNKS = (
    (0, 64, "S", 2),
    (64, 64, "Z", 2),
    (128, 64, "Z", 2),
    (192, 64, "Y", 4),
)
ORDER = (
    ("m", 0), ("F", 0), ("n", 0), ("F", 1), ("m", 1), ("n", 1), ("o", 1), ("N", 0), ("Y", 3), ("C", 0), ("C", 1),
    ("o", 0), ("F", 2), ("A", 0), ("A", 1), ("W", 3), ("E", 0), ("C", 2), ("E", 1), ("C", 3), ("P", 0), ("L", 0),
    ("A", 2), ("P", 1), ("E", 3), ("M", 0), ("E", 2), ("M", 1), ("L", 1), ("P", 2), ("L", 2), ("P", 3), ("M", 2),
    ("S", 1), ("L", 3), ("M", 3), ("R", 3), ("S", 0), ("K", 3), ("S", 2), ("S", 3),
)
CHUNKS_LAST = (
    (0, 64, "S", 2),
    (64, 64, "Z", 2),
    (128, 64, "Z", 2),
    (192, 64, "Y", 2),
)
ORDER_LAST = (
    ("m", 0), ("F", 0), ("n", 0), ("F", 1), ("m", 1), ("n", 1), ("o", 1), ("F", 2), ("Y", 3), ("C", 1), ("N", 0),
    ("C", 2), ("o", 0), ("C", 0), ("A", 1), ("W", 3), ("A", 2), ("A", 0), ("C", 3), ("E", 1), ("E", 2), ("E", 0),
    ("E", 3),
)
NQ = max(len(CHUNKS), len(CHUNKS_LAST))

TERM = {(0, 2): 0, (1, 1): 1, (1, 3): 2, (1, 0): 3, (1, 2): 4, (0, 3): 5, (0, 1): 6, (0, 0): 7}
UP, DOWN, DIR_UP, DIR_DOWN, COMB_UP, COMB_DOWN = range(6)
PARTNER, LEFT, RIGHT, LEFT_P, RIGHT_P, FAR, FAR_P = range(7)
PLACE = {PARTNER: (0, 1), LEFT: (3, 0), RIGHT: (1, 0), LEFT_P: (3, 1), RIGHT_P: (1, 1), FAR: (2, 0), FAR_P: (2, 1)}


def kernel(
    aff_hbm, col, lab, out,
    aff, lab_all, x0, x1, x2, p0, p1, p2, zin, yin, zout, yout, yall, ysum,
    aff_sem, lab_send, lab_recv, z_send, z_recv, y_recv, g_send, g_recv, s_recv,
):
    r, t = lax.axis_index("rep"), lax.axis_index("team")
    x, yh, c = r // 4, (r // 2) % 2, r % 2
    yl, z = t // 4, t % 4

    def rep_of(dx=0, dyh=0, dc=0):
        return lax.rem(x + dx, 4) * 4 + lax.rem(yh + dyh, 2) * 2 + lax.rem(c + dc, 2)

    def team_of(dyl=0, dz=0):
        return lax.rem(yl + dyl, 2) * 4 + lax.rem(z + dz, 4)

    above, below, beside = team_of(dz=1), team_of(dz=3), team_of(dyl=1)
    right, left, partner, twin = rep_of(dx=1), rep_of(dx=3), rep_of(dyh=1), rep_of(dc=1)

    def remote(src, dst, send, recv, rep=None, team=None):
        return pltpu.make_async_remote_copy(
            src_ref=src, dst_ref=dst, send_sem=send, recv_sem=recv,
            device_id={"team": t if team is None else team, "rep": r if rep is None else rep},
            device_id_type=MESH,
        )

    xs, ps = (x0, x1, x2), (p0, p1, p2)

    fetch = pltpu.make_async_copy(aff_hbm, aff, aff_sem)
    fetch.start()

    barrier = pltpu.get_barrier_semaphore()
    others = [(dc, dx, dyh) for dc in range(2) for dx in range(4) for dyh in range(2)][1:]
    for dc, dx, dyh in others:
        pl.semaphore_signal(
            barrier, inc=1, device_id={"team": t, "rep": rep_of(dx, dyh, dc)}, device_id_type=MESH
        )
    for other in (above, below, beside):
        pl.semaphore_signal(barrier, inc=1, device_id={"team": other, "rep": r}, device_id_type=MESH)
    pl.semaphore_wait(barrier, N_REP - 1 + 3)

    lab_copies = []
    for k, (dc, dx, dyh) in enumerate(others):
        at = dc * 8 + (4 - dx) % 4 * 2 + dyh
        lab_copies.append(
            remote(lab, lab_all.at[at], lab_send, lab_recv.at[k], rep=rep_of(dx, dyh, dc))
        )
        lab_copies[-1].start()
    channel = lax.broadcasted_iota(jnp.int32, (BLK, C), 1)

    def seed(at, rows_of):
        for h in range(2):
            x0[at // 2, at % 2, h] = jnp.where(rows_of(h)[:, None] == channel, 16.0, 0.0).astype(BF16)

    seed(0, lambda h: lab[h])
    for copy in lab_copies:
        copy.wait_recv()

    def seed_one(at, carry):
        seed(at, lambda h: lab_all[at, h])
        return carry

    lax.fori_loop(1, N_REP, seed_one, 0, unroll=3)
    fetch.wait()

    for it in range(ITERS):
        cur, p = xs[it], ps[it]
        nxt = xs[it + 1] if it + 1 < ITERS else None
        chunks, order = (CHUNKS, ORDER) if nxt is not None else (CHUNKS_LAST, ORDER_LAST)

        def picked(i, s, cur=cur):
            block = col[s, i]
            owner = lax.div(block, 2)
            dx = lax.rem(lax.div(owner, 4) + 4 - x, 4)
            dyh = lax.rem(lax.rem(lax.div(owner, 2), 2) + yh, 2)
            dc = lax.rem(lax.rem(owner, 2) + c, 2)
            return cur[dc * 4 + dx, dyh, lax.rem(block, 2)]

        def block_row(w, dz, h, p=p, picked=picked):
            i = 2 * team_of(w, dz) + h
            acc = None
            for s in range(0, KB, 2):
                lhs = jnp.concatenate([aff[i, s], aff[i, s + 1]], axis=1)
                rhs = jnp.concatenate([picked(i, s), picked(i, s + 1)], axis=0)
                d = jnp.dot(lhs, rhs, preferred_element_type=F32)
                acc = d if acc is None else acc + d
            p[TERM[w, dz], h * BLK : (h + 1) * BLK] = acc.astype(BF16)

        def products_far(h):
            for w in range(2):
                block_row(w, 2, h)

        def products_near(h):
            for dz in (1, 3):
                for w in range(2):
                    block_row(w, dz, h)

        def products_here(h):
            for w in range(2):
                block_row(w, 0, h)

        def rows(q):
            return pl.ds(chunks[q][0], chunks[q][1])

        def half(w, q):
            first, size = chunks[q][:2]
            return pl.ds(first + w * (size // 2), size // 2)

        def z_copy(kind, q):
            way, size = chunks[q][2], rows(q)
            if kind in (COMB_UP, COMB_DOWN):
                at = kind - COMB_UP
                part = half(at, q) if way == "Y" else size
                src, dst = zout.at[it, at, part], zin.at[it, kind, part]
            elif way == "Y":
                dz, part, at = {
                    UP: (2, 0, 0), DIR_UP: (1, 1, 1), DOWN: (2, 1, 2), DIR_DOWN: (3, 0, 3)
                }[kind]
                part = half(part, q)
                src, dst = ysum.at[it, dz, part], zin.at[it, at, part]
            else:
                first, at = {UP: (0, 0), DIR_UP: (1, 1), DOWN: (4, 2), DIR_DOWN: (5, 3)}[kind]
                if way == "Z":
                    src, dst = p.at[pl.ds(first, 2), size], zin.at[it, pl.ds(at, 2), size]
                else:
                    src, dst = p.at[first, size], zin.at[it, at, size]
            to = above if kind in (UP, DIR_UP, COMB_UP) else below
            return remote(src, dst, z_send.at[it], z_recv.at[it, q, kind], team=to)

        def far(q):
            z_copy(UP, q).start()
            z_copy(DOWN, q).start()

        def near(q):
            z_copy(DIR_UP, q).start()
            z_copy(DIR_DOWN, q).start()

        def combine(q):
            for w in range(2):
                z_copy((UP, DOWN)[w], q).wait_recv()
                if chunks[q][2] == "Y":
                    part = half(w, q)
                    mine = ysum[it, (1, 3)[w], part]
                else:
                    part = rows(q)
                    mine = p[TERM[w, (1, 3)[w]], part]
                total = mine.astype(F32) + zin[it, 2 * w, part].astype(F32)
                zout[it, w, part] = total.astype(BF16)
                z_copy((COMB_UP, COMB_DOWN)[w], q).start()

        def z_arrived(q):
            for w in range(2):
                if chunks[q][2] != "Z":
                    z_copy((DIR_UP, DIR_DOWN)[w], q).wait_recv()
                z_copy((COMB_UP, COMB_DOWN)[w], q).wait_recv()

        def z_sum(w, q):
            if chunks[q][2] == "Y":
                part = half(w, q)
                mine = ysum[it, 0, part]
            else:
                part = rows(q)
                mine = p[TERM[w, 0], part]
            return mine.astype(F32) + zin[it, (3, 1)[w], part].astype(F32) + zin[it, 4 + w, part].astype(F32)

        def y_copy(q):
            if chunks[q][2] == "Y":
                src, dst = p.at[pl.ds(1, 4), rows(q)], yall.at[it, :, rows(q)]
            else:
                src, dst = yout.at[it, rows(q)], yin.at[it, rows(q)]
            return remote(src, dst, z_send.at[it], y_recv.at[it, q], team=beside)

        def across(q):
            z_arrived(q)
            yout[it, rows(q)] = z_sum(1, q).astype(BF16)
            y_copy(q).start()

        def across_first(q):
            y_copy(q).start()

        def around(q):
            y_copy(q).wait_recv()
            for k, dz in enumerate((1, 3, 0, 2)):
                total = p[TERM[0, dz], rows(q)].astype(F32) + yall[it, k, rows(q)].astype(F32)
                ysum[it, dz, rows(q)] = total.astype(BF16)
            far(q)
            near(q)

        def spot(q):
            first, size = chunks[q][:2]
            return first // BLK, pl.ds(first % BLK, size)

        def g_copy(kind, q, of, to):
            h, at = spot(q)
            (sx, sy), (dx, dy) = of, PLACE[kind]
            return remote(
                nxt.at[sx, sy, h, at], nxt.at[dx, dy, h, at], g_send.at[it], g_recv.at[it, q, kind], rep=to
            )

        def s_copy(k, q):
            h, at = spot(q)
            first, count = (((0, 1), (1, 3)) if chunks[q][3] == 2 else ((0, 1), (3, 1), (1, 1), (2, 1)))[k]
            return remote(
                nxt.at[pl.ds(first, count), :, h, at], nxt.at[pl.ds(4 + first, count), :, h, at],
                g_send.at[it], s_recv.at[it, q, k], rep=twin,
            )

        def finish(q):
            if chunks[q][2] == "Y":
                z_arrived(q)
                sums = jnp.concatenate([z_sum(0, q), z_sum(1, q)], axis=0)
            else:
                y_copy(q).wait_recv()
                sums = z_sum(0, q) + yin[it, rows(q)].astype(F32)
            h, at = spot(q)
            seeded = x0[0, 0, h, at].astype(F32)
            blended = 0.9 * sums + 0.1 * seeded
            scale = lax.rsqrt(jnp.mean(blended * blended, axis=-1, keepdims=True) + 1e-6)
            scores = (blended * scale).astype(BF16)
            if nxt is None:
                out[rows(q)] = scores
                return
            nxt[0, 0, h, at] = scores
            g_copy(PARTNER, q, (0, 0), partner).start()
            g_copy(LEFT, q, (0, 0), right).start()
            g_copy(RIGHT, q, (0, 0), left).start()

        def got(kind, q):
            g_copy(kind, q, (0, 0), partner).wait_recv()

        def spread_partner(q):
            got(PARTNER, q)
            g_copy(LEFT_P, q, (0, 1), right).start()
            g_copy(RIGHT_P, q, (0, 1), left).start()
            s_copy(0, q).start()

        def spread_left(q):
            got(LEFT, q)
            g_copy(FAR, q, (3, 0), right).start()

        def spread_right(q):
            got(RIGHT_P, q)
            g_copy(FAR_P, q, (1, 1), left).start()

        def share_left(q):
            got(LEFT_P, q)
            s_copy(1, q).start()

        def share_right(q):
            got(RIGHT, q)
            s_copy(2, q).start()

        def share_far(q):
            kinds = (LEFT_P, RIGHT, FAR, FAR_P) if chunks[q][3] == 2 else (FAR, FAR_P)
            for kind in kinds:
                got(kind, q)
            s_copy(chunks[q][3] - 1, q).start()

        steps = dict(
            m=products_far, n=products_near, o=products_here, F=far, N=near, C=combine, A=across,
            Y=across_first, W=around, E=finish, P=spread_partner, L=spread_left, M=spread_right,
            K=share_left, R=share_right, S=share_far,
        )
        for step, q in order:
            steps[step](q)
        if nxt is not None:
            for q in range(len(chunks)):
                for k in range(chunks[q][3]):
                    s_copy(k, q).wait_recv()

    remote(lab_all.at[pl.ds(1, N_REP - 1)], lab_all.at[pl.ds(1, N_REP - 1)], lab_send, lab_recv.at[0], rep=twin).wait_send()
    for it in range(ITERS):
        sent = ps[it].at[pl.ds(0, 7)]
        remote(sent, sent, z_send.at[it], y_recv.at[it, 0], team=beside).wait_send()
        if it + 1 < ITERS:
            sent = zin.at[:, pl.ds(0, 5)]
            remote(sent, sent, g_send.at[it], g_recv.at[it, 0, 0], rep=twin).wait_send()


def on_device(affinity, col_index, labels):
    vmem = pl.BlockSpec(memory_space=pltpu.VMEM)
    dma = pltpu.SemaphoreType.DMA
    scores = pltpu.VMEM((8, 2, 2, BLK, C), BF16)
    partials = pltpu.VMEM((8, ROWS, C), BF16)
    return pl.pallas_call(
        kernel,
        out_shape=jax.ShapeDtypeStruct((ROWS, C), BF16),
        in_specs=[pl.BlockSpec(memory_space=pl.ANY), pl.BlockSpec(memory_space=pltpu.SMEM), vmem],
        out_specs=vmem,
        scratch_shapes=[
            pltpu.VMEM((16, KB, BLK, BLK), BF16),
            pltpu.VMEM((N_REP, 2, BLK), jnp.int32),
            scores, scores, scores,
            partials, partials, partials,
            pltpu.VMEM((ITERS, 6, ROWS, C), BF16),
            pltpu.VMEM((ITERS, ROWS, C), BF16),
            pltpu.VMEM((ITERS, 2, ROWS, C), BF16),
            pltpu.VMEM((ITERS, ROWS, C), BF16),
            pltpu.VMEM((ITERS, 4, ROWS, C), BF16),
            pltpu.VMEM((ITERS, 4, ROWS, C), BF16),
            dma,
            dma, dma((N_REP - 1,)),
            dma((ITERS,)), dma((ITERS, NQ, 6)),
            dma((ITERS, NQ)),
            dma((ITERS - 1,)), dma((ITERS - 1, NQ, 7)),
            dma((ITERS - 1, NQ, 4)),
        ],
        compiler_params=pltpu.CompilerParams(
            collective_id=0, has_side_effects=True, vmem_limit_bytes=60 * 2**20
        ),
    )(affinity[0], col_index[0].T, labels.reshape(2, BLK))


def solution(mesh):
    in_specs = (P("team", "rep", None, None, None), P("team", "rep", None), P(("rep", "team")))
    out_specs = P(("rep", "team"), None)
    return jax.shard_map(
        on_device, mesh=mesh, in_specs=in_specs, out_specs=out_specs, check_vma=False
    )
```

time: 506 us -> 110 us (0.22)
  waiting for transfers between devices: 290 us -> 0 us
  Pallas kernels: 0 us -> 108 us
  local copies, waits for them, and re-layouts: 108 us -> 1.67 us
  matrix products: 82.3 us -> 0 us
  between operations: 13.6 us -> 0.01 us
  other arithmetic: 10.8 us -> 0 us
    all_gather x3 -> x0, waiting for transfers between devices: 164 us -> none  [on_device(): lax.all_gather(current, 'rep', axis=0, tiled=True).reshape(-1, block, C)]
    reduce_scatter x3 -> x0, waiting for transfers between devices: 125 us -> none  [on_device(): lax.psum_scatter(summed.reshape(lax.axis_size('team') * rows_here, C).ast...]
    pallas_call x0 -> x1, Pallas kernels: none -> 108 us  [on_device(): pl.pallas_call(kernel, out_shape=jax.ShapeDtypeStruct((ROWS, C), BF16), i...]
    gather x24 -> x0, local copies, waits for them, and re-layouts: 96.9 us -> none  [on_device(): picked = gathered[columns[:, slot_index]]]
    dot_general x24 -> x0, matrix products: 82.3 us -> none  [on_device(): jnp.einsum('iab,ibc->iac', panels[:, slot_index], picked, preferred_eleme...]
    unnamed x47 -> x1, local copies, waits for them, and re-layouts: 10.7 us -> 1.67 us
    convert_element_type x4 -> x0, other arithmetic: 7.05 us -> none  [the longest x3 5.56 us: on_device(): current = (blended * scale_rows).astype(jnp.bfloat16)]
  transfers between devices with their start and end apart: 6 -> 0, of which waited for: 6 -> 0; matrix products, arithmetic and copies ran while one was open for 1% -> 0% of each run, Pallas kernels for 0% -> 0%
where the time goes in v3:
time: 110 us; the launch traced here: 109 us
  Pallas kernels  108 us (98%)
  local copies, waits for them, and re-layouts  1.67 us (2%)
    pallas_call x1, Pallas kernels, on_device(): pl.pallas_call(kernel, out_shape=jax.ShapeDtypeStruct((ROWS, C), BF16), i...  108 us

profile of v3, /device:TPU:0, one launch (start us, length us, event | category | flops | bytes accessed | tf_op | source)
XLA Modules:
  0.0 109.2 jit_solution(16635071648803738392)
XLA Ops:
  0.0 107.5 %shard_map.37 = bf16[256,512]{1,0:T(8,128)(2,1)} custom-call(bf16[16,8,128,128]{3,2,1,0:T(8,128)(2,1)} %bitcast.5, s32[8,16]{1,0:T(8,128)} %bitcast.6, s32[2,128]{1,0:T(2,128)} %bitcast.7), custom_call_target="tpu_custom_call" | custom-call | tf_op jit(solution)/shard_map/pallas_call | solution.py:334
  107.5 1.7 %copy.5 = bf16[256,512]{1,0:T(8,128)(2,1)} copy(bf16[256,512]{1,0:T(8,128)(2,1)} %shard_map.37) | data formatting | bytes 524288

commit v4 on v3

v4 whole, which is shorter than its diff:
```python
import functools

import jax
import jax.numpy as jnp
from jax import lax
from jax.experimental import pallas as pl
from jax.experimental.pallas import tpu as pltpu
from jax.sharding import PartitionSpec as P

C = 512
BLK = 128
KB = 8
ITERS = 3
ROWS = 256
N_REP = 16
MESH = pl.DeviceIdType.MESH
F32 = jnp.float32
BF16 = jnp.bfloat16

CHUNKS = (
    (0, 128, "S", 2, 0),
    (128, 128, "Z", 2, 0),
    (0, 128, "Z", 2, 1),
    (128, 128, "Z", 2, 1),
)
ORDER = (
    ("m", 0, 0), ("F", 0, 0), ("n", 0, 0), ("F", 0, 1), ("C", 0, 0), ("o", 0, 0), ("m", 0, 1), ("N", 0, 0),
    ("C", 0, 1), ("n", 0, 1), ("F", 0, 2), ("A", 0, 0), ("A", 0, 1), ("F", 0, 3), ("E", 0, 0), ("C", 0, 2),
    ("E", 0, 1), ("o", 0, 1), ("C", 0, 3), ("P", 0, 0), ("A", 0, 2), ("L", 0, 1), ("P", 0, 1), ("L", 0, 0),
    ("A", 0, 3), ("M", 0, 0), ("M", 0, 1), ("E", 0, 2), ("E", 0, 3), ("V", 0, 0), ("S", 0, 0), ("S", 0, 1),
    ("P", 0, 2), ("P", 0, 3), ("L", 0, 2), ("X", 0, 0), ("L", 0, 3), ("U", 0, 0), ("M", 0, 2), ("m", 1, 0),
    ("F", 1, 0), ("M", 0, 3), ("n", 1, 0), ("F", 1, 1), ("S", 0, 2), ("S", 0, 3), ("N", 1, 0), ("C", 1, 0),
    ("o", 1, 0), ("X", 0, 1), ("m", 1, 1), ("C", 1, 1), ("n", 1, 1), ("F", 1, 2), ("A", 1, 0), ("A", 1, 1),
    ("F", 1, 3), ("E", 1, 0), ("C", 1, 2), ("E", 1, 1), ("o", 1, 1), ("C", 1, 3), ("P", 1, 0), ("L", 1, 0),
    ("A", 1, 2), ("P", 1, 1), ("L", 1, 1), ("A", 1, 3), ("M", 1, 0), ("M", 1, 1), ("E", 1, 2), ("E", 1, 3),
    ("V", 1, 0), ("S", 1, 0), ("S", 1, 1), ("P", 1, 2), ("L", 1, 2), ("P", 1, 3), ("X", 1, 0), ("L", 1, 3),
    ("U", 1, 0), ("M", 1, 2), ("m", 2, 0), ("F", 2, 0), ("M", 1, 3), ("n", 2, 0), ("F", 2, 1), ("S", 1, 2),
    ("S", 1, 3), ("N", 2, 0), ("C", 2, 0), ("o", 2, 0), ("X", 1, 1), ("m", 2, 1), ("C", 2, 1), ("n", 2, 1),
    ("F", 2, 3), ("A", 2, 0), ("o", 2, 1), ("F", 2, 2), ("C", 2, 3), ("A", 2, 1), ("C", 2, 2), ("A", 2, 3),
    ("E", 2, 0), ("E", 2, 1), ("A", 2, 2), ("E", 2, 3), ("E", 2, 2), ("V", 2, 0),
)
NQ = len(CHUNKS)
HALF = C // 2

TERM = {(0, 2): 0, (1, 1): 1, (1, 3): 2, (1, 0): 3, (1, 2): 4, (0, 3): 5, (0, 1): 6, (0, 0): 7}
UP, DOWN, DIR_UP, DIR_DOWN, COMB_UP, COMB_DOWN = range(6)
PARTNER, LEFT, RIGHT, LEFT_P, RIGHT_P, FAR, FAR_P = range(7)
PLACE = {PARTNER: (0, 1), LEFT: (3, 0), RIGHT: (1, 0), LEFT_P: (3, 1), RIGHT_P: (1, 1), FAR: (2, 0), FAR_P: (2, 1)}


def kernel(
    aff_hbm, col, lab, out,
    aff, scaled, lab_all, x0a, x0b, x1a, x1b, x2a, x2b, p0, p1, p2, zin, yin, zout, yout, yall, ysum, squares, kept,
    scale0, scale1,
    aff_sem, lab_send, lab_recv, z_send, z_recv, y_recv, g_send, g_recv, s_recv, v_send, v_recv,
):
    r, t = lax.axis_index("rep"), lax.axis_index("team")
    x, yh, c = r // 4, (r // 2) % 2, r % 2
    yl, z = t // 4, t % 4

    def rep_of(dx=0, dyh=0, dc=0):
        return lax.rem(x + dx, 4) * 4 + lax.rem(yh + dyh, 2) * 2 + lax.rem(c + dc, 2)

    def team_of(dyl=0, dz=0):
        return lax.rem(yl + dyl, 2) * 4 + lax.rem(z + dz, 4)

    above, below, beside = team_of(dz=1), team_of(dz=3), team_of(dyl=1)
    right, left, partner, twin = rep_of(dx=1), rep_of(dx=3), rep_of(dyh=1), rep_of(dc=1)

    def remote(src, dst, send, recv, rep=None, team=None):
        return pltpu.make_async_remote_copy(
            src_ref=src, dst_ref=dst, send_sem=send, recv_sem=recv,
            device_id={"team": t if team is None else team, "rep": r if rep is None else rep},
            device_id_type=MESH,
        )

    xs, ps, scales = ((x0a, x0b), (x1a, x1b), (x2a, x2b)), (p0, p1, p2), (scale0, scale1)

    fetch = pltpu.make_async_copy(aff_hbm, aff, aff_sem)
    fetch.start()

    barrier = pltpu.get_barrier_semaphore()
    others = [(dc, dx, dyh) for dc in range(2) for dx in range(4) for dyh in range(2)][1:]
    others.sort(key=lambda o: -min(o[1], 4 - o[1]) - 2 * o[2])
    for dc, dx, dyh in others:
        pl.semaphore_signal(
            barrier, inc=1, device_id={"team": t, "rep": rep_of(dx, dyh, dc)}, device_id_type=MESH
        )
    for other in (above, below, beside):
        pl.semaphore_signal(barrier, inc=1, device_id={"team": other, "rep": r}, device_id_type=MESH)
    pl.semaphore_wait(barrier, N_REP - 1 + 3)

    lab_copies = []
    for k, (dc, dx, dyh) in enumerate(others):
        at = dc * 8 + (4 - dx) % 4 * 2 + dyh
        lab_copies.append(
            remote(lab, lab_all.at[at], lab_send, lab_recv.at[k], rep=rep_of(dx, dyh, dc))
        )
        lab_copies[-1].start()
    channel = lax.broadcasted_iota(jnp.int32, (BLK, HALF), 1)

    def seed(at, rows_of):
        for h in range(2):
            label = rows_of(h)[:, None]
            for n in range(2):
                x0 = xs[0][n]
                x0[at // 2, at % 2, h] = jnp.where(label == channel + n * HALF, 16.0, 0.0).astype(BF16)

    seed(0, lambda h: lab[h])
    for copy in lab_copies:
        copy.wait_recv()

    def seed_one(at, carry):
        seed(at, lambda h: lab_all[at, h])
        return carry

    lax.fori_loop(1, N_REP, seed_one, 0, unroll=3)
    fetch.wait()

    def steps_of(it):
        p = ps[it]
        nxt = xs[it + 1] if it + 1 < ITERS else None
        chunks = CHUNKS

        def place_of(i, s):
            block = col[s, i]
            owner = lax.div(block, 2)
            dx = lax.rem(lax.div(owner, 4) + 4 - x, 4)
            dyh = lax.rem(lax.rem(lax.div(owner, 2), 2) + yh, 2)
            dc = lax.rem(lax.rem(owner, 2) + c, 2)
            return dc * 4 + dx, dyh, lax.rem(block, 2)

        def block_row(w, dz, h, n):
            i = 2 * team_of(w, dz) + h
            cur = xs[it][n]
            places = [place_of(i, s) for s in range(KB)]

            def weights(s):
                if it == 0:
                    return aff[i, s]
                if n == 1:
                    return scaled[TERM[w, dz], h, s]
                a, b, k = places[s]
                by = scales[it - 1][2 * a + b, pl.ds(k, 1)]
                product = (aff[i, s].astype(F32) * by).astype(BF16)
                scaled[TERM[w, dz], h, s] = product
                return product

            acc = None
            for s in range(0, KB, 2):
                lhs = jnp.concatenate([weights(s), weights(s + 1)], axis=1)
                rhs = jnp.concatenate([cur[places[s]], cur[places[s + 1]]], axis=0)
                d = jnp.dot(lhs, rhs, preferred_element_type=F32)
                acc = d if acc is None else acc + d
            p[n, TERM[w, dz], h * BLK : (h + 1) * BLK] = acc.astype(BF16)

        def products(dzs, n):
            for dz in dzs:
                for h in range(2):
                    for w in range(2):
                        block_row(w, dz, h, n)

        def n_of(q):
            return chunks[q][4]

        def rows(q):
            return pl.ds(chunks[q][0], chunks[q][1])

        def half(w, q):
            first, size = chunks[q][:2]
            return pl.ds(first + w * (size // 2), size // 2)

        def z_copy(kind, q):
            way, size, n = chunks[q][2], rows(q), n_of(q)
            if kind in (COMB_UP, COMB_DOWN):
                at = kind - COMB_UP
                part = half(at, q) if way == "Y" else size
                src, dst = zout.at[it, n, at, part], zin.at[it, n, kind, part]
            elif way == "Y":
                dz, part, at = {
                    UP: (2, 0, 0), DIR_UP: (1, 1, 1), DOWN: (2, 1, 2), DIR_DOWN: (3, 0, 3)
                }[kind]
                part = half(part, q)
                src, dst = ysum.at[it, n, dz, part], zin.at[it, n, at, part]
            else:
                first, at = {UP: (0, 0), DIR_UP: (1, 1), DOWN: (4, 2), DIR_DOWN: (5, 3)}[kind]
                if way == "Z":
                    src, dst = p.at[n, pl.ds(first, 2), size], zin.at[it, n, pl.ds(at, 2), size]
                else:
                    src, dst = p.at[n, first, size], zin.at[it, n, at, size]
            to = above if kind in (UP, DIR_UP, COMB_UP) else below
            return remote(src, dst, z_send.at[it], z_recv.at[it, q, kind], team=to)

        def far(q):
            z_copy(UP, q).start()
            z_copy(DOWN, q).start()

        def near(q):
            z_copy(DIR_UP, q).start()
            z_copy(DIR_DOWN, q).start()

        def combine(q):
            for w in range(2):
                z_copy((UP, DOWN)[w], q).wait_recv()
                if chunks[q][2] == "Y":
                    part = half(w, q)
                    mine = ysum[it, n_of(q), (1, 3)[w], part]
                else:
                    part = rows(q)
                    mine = p[n_of(q), TERM[w, (1, 3)[w]], part]
                total = mine.astype(F32) + zin[it, n_of(q), 2 * w, part].astype(F32)
                zout[it, n_of(q), w, part] = total.astype(BF16)
                z_copy((COMB_UP, COMB_DOWN)[w], q).start()

        def z_arrived(q):
            for w in range(2):
                if chunks[q][2] != "Z":
                    z_copy((DIR_UP, DIR_DOWN)[w], q).wait_recv()
                z_copy((COMB_UP, COMB_DOWN)[w], q).wait_recv()

        def z_sum(w, q):
            if chunks[q][2] == "Y":
                part = half(w, q)
                mine = ysum[it, n_of(q), 0, part]
            else:
                part = rows(q)
                mine = p[n_of(q), TERM[w, 0], part]
            arrived = [zin[it, n_of(q), k, part].astype(F32) for k in ((3, 1)[w], 4 + w)]
            return mine.astype(F32) + arrived[0] + arrived[1]

        def y_copy(q):
            if chunks[q][2] == "Y":
                src, dst = p.at[n_of(q), pl.ds(1, 4), rows(q)], yall.at[it, n_of(q), :, rows(q)]
            else:
                src, dst = yout.at[it, n_of(q), rows(q)], yin.at[it, n_of(q), rows(q)]
            return remote(src, dst, z_send.at[it], y_recv.at[it, q], team=beside)

        def across(q):
            z_arrived(q)
            yout[it, n_of(q), rows(q)] = z_sum(1, q).astype(BF16)
            y_copy(q).start()

        def across_first(q):
            y_copy(q).start()

        def around(q):
            y_copy(q).wait_recv()
            for k, dz in enumerate((1, 3, 0, 2)):
                total = p[n_of(q), TERM[0, dz], rows(q)].astype(F32) + yall[it, n_of(q), k, rows(q)].astype(F32)
                ysum[it, n_of(q), dz, rows(q)] = total.astype(BF16)
            far(q)
            near(q)

        def spot(q):
            first, size = chunks[q][:2]
            return first // BLK, pl.ds(first % BLK, size)

        def g_copy(kind, q, of, to):
            h, at = spot(q)
            (sx, sy), (dx, dy) = of, PLACE[kind]
            return remote(
                nxt[n_of(q)].at[sx, sy, h, at], nxt[n_of(q)].at[dx, dy, h, at], g_send.at[it], g_recv.at[it, q, kind], rep=to
            )

        def s_copy(k, q):
            h, at = spot(q)
            first, count = (((0, 1), (1, 3)) if chunks[q][3] == 2 else ((0, 1), (3, 1), (1, 1), (2, 1)))[k]
            return remote(
                nxt[n_of(q)].at[pl.ds(first, count), :, h, at], nxt[n_of(q)].at[pl.ds(4 + first, count), :, h, at],
                g_send.at[it], s_recv.at[it, q, k], rep=twin,
            )

        def finish(q):
            if chunks[q][2] == "Y":
                z_arrived(q)
                sums = jnp.concatenate([z_sum(0, q), z_sum(1, q)], axis=0)
            else:
                y_copy(q).wait_recv()
                sums = z_sum(0, q) + yin[it, n_of(q), rows(q)].astype(F32)
            h, at = spot(q)
            seeded = xs[0][n_of(q)][0, 0, h, at].astype(F32)
            blended = 0.9 * sums + 0.1 * seeded
            left_half, right_half = blended[:, : HALF // 2], blended[:, HALF // 2 :]
            squares[n_of(q), rows(q)] = left_half * left_half + right_half * right_half
            if nxt is None:
                kept[n_of(q), rows(q)] = blended
                return
            nxt[n_of(q)][0, 0, h, at] = blended.astype(BF16)
            g_copy(PARTNER, q, (0, 0), partner).start()
            g_copy(LEFT, q, (0, 0), right).start()
            g_copy(RIGHT, q, (0, 0), left).start()

        def got(kind, q):
            g_copy(kind, q, (0, 0), partner).wait_recv()

        def spread_partner(q):
            got(PARTNER, q)
            g_copy(LEFT_P, q, (0, 1), right).start()
            g_copy(RIGHT_P, q, (0, 1), left).start()
            s_copy(0, q).start()

        def spread_left(q):
            got(LEFT, q)
            g_copy(FAR, q, (3, 0), right).start()

        def spread_right(q):
            got(RIGHT_P, q)
            g_copy(FAR_P, q, (1, 1), left).start()

        def share_left(q):
            got(LEFT_P, q)
            s_copy(1, q).start()

        def share_right(q):
            got(RIGHT, q)
            s_copy(2, q).start()

        def share_far(q):
            kinds = (LEFT_P, RIGHT, FAR, FAR_P) if chunks[q][3] == 2 else (FAR, FAR_P)
            for kind in kinds:
                got(kind, q)
            s_copy(chunks[q][3] - 1, q).start()

        def v_copy(k):
            dc, dx, dyh = others[k]
            at = dc * 8 + (4 - dx) % 4 * 2 + dyh
            own = scales[it].at[0]
            return remote(own, scales[it].at[at], v_send.at[it], v_recv.at[it, k], rep=rep_of(dx, dyh, dc))

        def send_scales(_):
            diagonal = lax.broadcasted_iota(jnp.int32, (BLK, BLK), 0) == lax.broadcasted_iota(jnp.int32, (BLK, BLK), 1)
            for h in range(2):
                at = pl.ds(h * BLK, BLK)
                mean = jnp.sum(squares[0, at] + squares[1, at], axis=-1, keepdims=True) / C
                scale = lax.rsqrt(mean + 1e-6)
                if nxt is None:
                    for n in range(2):
                        out[at, n * HALF : (n + 1) * HALF] = (kept[n, at] * scale).astype(BF16)
                else:
                    scales[it][0, pl.ds(h, 1)] = jnp.sum(jnp.where(diagonal, scale, 0.0), axis=0, keepdims=True)
            if nxt is not None:
                for k in range(N_REP - 1):
                    v_copy(k).start()

        def take_scales(_):
            for k in range(N_REP - 1):
                v_copy(k).wait_recv()

        def take_shares(n):
            for q in range(NQ):
                if n_of(q) == n:
                    for k in range(chunks[q][3]):
                        s_copy(k, q).wait_recv()

        return dict(
            m=functools.partial(products, (2,)), n=functools.partial(products, (1, 3)), o=functools.partial(products, (0,)),
            F=far, N=near, C=combine, A=across, Y=across_first, W=around, E=finish,
            P=spread_partner, L=spread_left, M=spread_right, K=share_left, R=share_right, S=share_far,
            V=send_scales, U=take_scales, X=take_shares,
        )

    steps = [steps_of(it) for it in range(ITERS)]
    for step, it, q in ORDER:
        steps[it][step](q)

    remote(lab_all.at[pl.ds(1, N_REP - 1)], lab_all.at[pl.ds(1, N_REP - 1)], lab_send, lab_recv.at[0], rep=twin).wait_send()
    for it in range(ITERS):
        sent = ps[it].at[:, pl.ds(0, 7)]
        remote(sent, sent, z_send.at[it], y_recv.at[it, 0], team=beside).wait_send()
        if it + 1 < ITERS:
            sent = zin.at[:, :, pl.ds(0, 5)]
            remote(sent, sent, g_send.at[it], g_recv.at[it, 0, 0], rep=twin).wait_send()
            sent = scales[it].at[pl.ds(1, N_REP - 1)]
            remote(sent, sent, v_send.at[it], v_recv.at[it, 0], rep=twin).wait_send()


def on_device(affinity, col_index, labels):
    vmem = pl.BlockSpec(memory_space=pltpu.VMEM)
    dma = pltpu.SemaphoreType.DMA
    scores = pltpu.VMEM((8, 2, 2, BLK, HALF), BF16)
    partials = pltpu.VMEM((2, 8, ROWS, HALF), BF16)
    return pl.pallas_call(
        kernel,
        out_shape=jax.ShapeDtypeStruct((ROWS, C), BF16),
        in_specs=[pl.BlockSpec(memory_space=pl.ANY), pl.BlockSpec(memory_space=pltpu.SMEM), vmem],
        out_specs=vmem,
        scratch_shapes=[
            pltpu.VMEM((16, KB, BLK, BLK), BF16),
            pltpu.VMEM((8, 2, KB, BLK, BLK), BF16),
            pltpu.VMEM((N_REP, 2, BLK), jnp.int32),
            scores, scores, scores, scores, scores, scores,
            partials, partials, partials,
            pltpu.VMEM((ITERS, 2, 6, ROWS, HALF), BF16),
            pltpu.VMEM((ITERS, 2, ROWS, HALF), BF16),
            pltpu.VMEM((ITERS, 2, 2, ROWS, HALF), BF16),
            pltpu.VMEM((ITERS, 2, ROWS, HALF), BF16),
            pltpu.VMEM((ITERS, 2, 4, ROWS, HALF), BF16),
            pltpu.VMEM((ITERS, 2, 4, ROWS, HALF), BF16),
            pltpu.VMEM((2, ROWS, HALF // 2), F32),
            pltpu.VMEM((2, ROWS, HALF), F32),
            pltpu.VMEM((N_REP, 2, BLK), F32), pltpu.VMEM((N_REP, 2, BLK), F32),
            dma,
            dma, dma((N_REP - 1,)),
            dma((ITERS,)), dma((ITERS, NQ, 6)),
            dma((ITERS, NQ)),
            dma((ITERS - 1,)), dma((ITERS - 1, NQ, 7)),
            dma((ITERS - 1, NQ, 4)),
            dma((ITERS - 1,)), dma((ITERS - 1, N_REP - 1)),
        ],
        compiler_params=pltpu.CompilerParams(
            collective_id=0, has_side_effects=True, vmem_limit_bytes=60 * 2**20
        ),
    )(affinity[0], col_index[0].T, labels.reshape(2, BLK))


def solution(mesh):
    in_specs = (P("team", "rep", None, None, None), P("team", "rep", None), P(("rep", "team")))
    out_specs = P(("rep", "team"), None)
    return jax.shard_map(
        on_device, mesh=mesh, in_specs=in_specs, out_specs=out_specs, check_vma=False
    )
```

time: 110 us -> 108 us (0.982)
  Pallas kernels: 108 us -> 106 us
    pallas_call x1, Pallas kernels: 108 us -> 106 us  [on_device(): pl.pallas_call(kernel, out_shape=jax.ShapeDtypeStruct((ROWS, C), BF16), i...]
where the time goes in v4:
time: 108 us
  Pallas kernels  106 us (98%)
  local copies, waits for them, and re-layouts  1.67 us (2%)
    pallas_call x1, Pallas kernels, on_device(): pl.pallas_call(kernel, out_shape=jax.ShapeDtypeStruct((ROWS, C), BF16), i...  106 us

profile of v4, /device:TPU:0, one launch (start us, length us, event | category | flops | bytes accessed | tf_op | source)
XLA Modules:
  0.0 107.7 jit_solution(9375667957360534024)
XLA Ops:
  0.0 106.0 %shard_map.37 = bf16[256,512]{1,0:T(8,128)(2,1)} custom-call(bf16[16,8,128,128]{3,2,1,0:T(8,128)(2,1)} %bitcast.5, s32[8,16]{1,0:T(8,128)} %bitcast.6, s32[2,128]{1,0:T(2,128)} %bitcast.7), custom_call_target="tpu_custom_call" | custom-call | tf_op jit(solution)/shard_map/pallas_call | solution.py:382
  106.0 1.7 %copy.5 = bf16[256,512]{1,0:T(8,128)(2,1)} copy(bf16[256,512]{1,0:T(8,128)(2,1)} %shard_map.37) | data formatting | bytes 524288

commit v5 on v4

--- a/solution.py
+++ b/solution.py
@@ -18,28 +18,28 @@
 BF16 = jnp.bfloat16
 
 CHUNKS = (
-    (0, 128, "S", 2, 0),
-    (128, 128, "Z", 2, 0),
-    (0, 128, "Z", 2, 1),
-    (128, 128, "Z", 2, 1),
+    ((0, 128, "S", 2, 0), (128, 128, "S", 2, 0), (0, 128, "S", 2, 1), (128, 128, "S", 2, 1),),
+    ((0, 128, "S", 2, 0), (128, 128, "S", 2, 0), (0, 128, "S", 2, 1), (128, 128, "S", 2, 1),),
+    ((0, 128, "S", 2, 0), (128, 128, "Z", 2, 0), (0, 128, "Y", 2, 1), (128, 128, "Z", 2, 1),),
 )
 ORDER = (
-    ("m", 0, 0), ("F", 0, 0), ("n", 0, 0), ("F", 0, 1), ("C", 0, 0), ("o", 0, 0), ("m", 0, 1), ("N", 0, 0),
-    ("C", 0, 1), ("n", 0, 1), ("F", 0, 2), ("A", 0, 0), ("A", 0, 1), ("F", 0, 3), ("E", 0, 0), ("C", 0, 2),
-    ("E", 0, 1), ("o", 0, 1), ("C", 0, 3), ("P", 0, 0), ("A", 0, 2), ("L", 0, 1), ("P", 0, 1), ("L", 0, 0),
-    ("A", 0, 3), ("M", 0, 0), ("M", 0, 1), ("E", 0, 2), ("E", 0, 3), ("V", 0, 0), ("S", 0, 0), ("S", 0, 1),
-    ("P", 0, 2), ("P", 0, 3), ("L", 0, 2), ("X", 0, 0), ("L", 0, 3), ("U", 0, 0), ("M", 0, 2), ("m", 1, 0),
-    ("F", 1, 0), ("M", 0, 3), ("n", 1, 0), ("F", 1, 1), ("S", 0, 2), ("S", 0, 3), ("N", 1, 0), ("C", 1, 0),
-    ("o", 1, 0), ("X", 0, 1), ("m", 1, 1), ("C", 1, 1), ("n", 1, 1), ("F", 1, 2), ("A", 1, 0), ("A", 1, 1),
-    ("F", 1, 3), ("E", 1, 0), ("C", 1, 2), ("E", 1, 1), ("o", 1, 1), ("C", 1, 3), ("P", 1, 0), ("L", 1, 0),
-    ("A", 1, 2), ("P", 1, 1), ("L", 1, 1), ("A", 1, 3), ("M", 1, 0), ("M", 1, 1), ("E", 1, 2), ("E", 1, 3),
-    ("V", 1, 0), ("S", 1, 0), ("S", 1, 1), ("P", 1, 2), ("L", 1, 2), ("P", 1, 3), ("X", 1, 0), ("L", 1, 3),
-    ("U", 1, 0), ("M", 1, 2), ("m", 2, 0), ("F", 2, 0), ("M", 1, 3), ("n", 2, 0), ("F", 2, 1), ("S", 1, 2),
-    ("S", 1, 3), ("N", 2, 0), ("C", 2, 0), ("o", 2, 0), ("X", 1, 1), ("m", 2, 1), ("C", 2, 1), ("n", 2, 1),
-    ("F", 2, 3), ("A", 2, 0), ("o", 2, 1), ("F", 2, 2), ("C", 2, 3), ("A", 2, 1), ("C", 2, 2), ("A", 2, 3),
-    ("E", 2, 0), ("E", 2, 1), ("A", 2, 2), ("E", 2, 3), ("E", 2, 2), ("V", 2, 0),
+    ("m", 0, 0), ("F", 0, 0), ("n", 0, 0), ("F", 0, 1), ("N", 0, 0), ("o", 0, 0), ("m", 0, 1), ("N", 0, 1),
+    ("C", 0, 0), ("C", 0, 1), ("n", 0, 1), ("F", 0, 2), ("A", 0, 0), ("N", 0, 2), ("F", 0, 3), ("A", 0, 1),
+    ("N", 0, 3), ("E", 0, 0), ("C", 0, 2), ("E", 0, 1), ("o", 0, 1), ("C", 0, 3), ("P", 0, 0), ("A", 0, 2),
+    ("P", 0, 1), ("L", 0, 1), ("L", 0, 0), ("A", 0, 3), ("M", 0, 0), ("M", 0, 1), ("E", 0, 2), ("E", 0, 3),
+    ("V", 0, 0), ("S", 0, 0), ("S", 0, 1), ("P", 0, 2), ("P", 0, 3), ("L", 0, 2), ("L", 0, 3), ("X", 0, 0),
+    ("U", 0, 0), ("m", 1, 0), ("F", 1, 0), ("M", 0, 2), ("n", 1, 0), ("F", 1, 1), ("M", 0, 3), ("N", 1, 0),
+    ("C", 1, 0), ("S", 0, 2), ("S", 0, 3), ("N", 1, 1), ("C", 1, 1), ("o", 1, 0), ("X", 0, 1), ("m", 1, 1),
+    ("F", 1, 2), ("A", 1, 0), ("F", 1, 3), ("n", 1, 1), ("N", 1, 3), ("A", 1, 1), ("N", 1, 2), ("E", 1, 0),
+    ("C", 1, 2), ("o", 1, 1), ("E", 1, 1), ("C", 1, 3), ("L", 1, 0), ("P", 1, 0), ("A", 1, 2), ("P", 1, 1),
+    ("A", 1, 3), ("L", 1, 1), ("M", 1, 0), ("E", 1, 2), ("M", 1, 1), ("E", 1, 3), ("V", 1, 0), ("P", 1, 2),
+    ("S", 1, 0), ("L", 1, 3), ("L", 1, 2), ("P", 1, 3), ("S", 1, 1), ("U", 1, 0), ("M", 1, 2), ("X", 1, 0),
+    ("M", 1, 3), ("m", 2, 0), ("F", 2, 0), ("n", 2, 0), ("S", 1, 2), ("N", 2, 0), ("S", 1, 3), ("o", 2, 0),
+    ("F", 2, 1), ("C", 2, 0), ("X", 1, 1), ("m", 2, 1), ("n", 2, 1), ("o", 2, 1), ("Y", 2, 2), ("F", 2, 3),
+    ("C", 2, 1), ("C", 2, 3), ("A", 2, 0), ("A", 2, 1), ("W", 2, 2), ("A", 2, 3), ("C", 2, 2), ("E", 2, 0),
+    ("E", 2, 1), ("E", 2, 3), ("E", 2, 2), ("V", 2, 0),
 )
-NQ = len(CHUNKS)
+NQ = len(CHUNKS[0])
 HALF = C // 2
 
 TERM = {(0, 2): 0, (1, 1): 1, (1, 3): 2, (1, 0): 3, (1, 2): 4, (0, 3): 5, (0, 1): 6, (0, 0): 7}
@@ -107,20 +107,17 @@
                 x0[at // 2, at % 2, h] = jnp.where(label == channel + n * HALF, 16.0, 0.0).astype(BF16)
 
     seed(0, lambda h: lab[h])
-    for copy in lab_copies:
-        copy.wait_recv()
-
-    def seed_one(at, carry):
-        seed(at, lambda h: lab_all[at, h])
-        return carry
-
-    lax.fori_loop(1, N_REP, seed_one, 0, unroll=3)
+    for k in reversed(range(N_REP - 1)):
+        dc, dx, dyh = others[k]
+        at = dc * 8 + (4 - dx) % 4 * 2 + dyh
+        lab_copies[k].wait_recv()
+        seed(at, lambda h, at=at: lab_all[at, h])
     fetch.wait()
 
     def steps_of(it):
         p = ps[it]
         nxt = xs[it + 1] if it + 1 < ITERS else None
-        chunks = CHUNKS
+        chunks = CHUNKS[it]
 
         def place_of(i, s):
             block = col[s, i]
@@ -408,7 +405,7 @@
             dma((ITERS - 1,)), dma((ITERS - 1, N_REP - 1)),
         ],
         compiler_params=pltpu.CompilerParams(
-            collective_id=0, has_side_effects=True, vmem_limit_bytes=60 * 2**20
+            collective_id=0, has_side_effects=True, vmem_limit_bytes=50 * 2**20
         ),
     )(affinity[0], col_index[0].T, labels.reshape(2, BLK))
 

time: 108 us -> 104 us (0.963)
  Pallas kernels: 106 us -> 102 us
    pallas_call x1, Pallas kernels: 106 us -> 102 us  [on_device(): pl.pallas_call(kernel, out_shape=jax.ShapeDtypeStruct((ROWS, C), BF16), i...]
where the time goes in v5:
time: 104 us
  Pallas kernels  102 us (98%)
  local copies, waits for them, and re-layouts  2.07 us (2%)
    pallas_call x1, Pallas kernels, on_device(): pl.pallas_call(kernel, out_shape=jax.ShapeDtypeStruct((ROWS, C), BF16), i...  102 us

profile of v5, /device:TPU:0, one launch (start us, length us, event | category | flops | bytes accessed | tf_op | source)
XLA Modules:
  0.0 104.3 jit_solution(8573917008460941431)
XLA Ops:
  0.0 0.0 copy-start
  0.0 0.7 copy-done
  0.7 0.0 copy-start.1
  0.7 0.7 copy-done.1
  1.4 102.2 %shard_map.37 = bf16[256,512]{1,0:T(8,128)(2,1)S(1)} custom-call(bf16[16,8,128,128]{3,2,1,0:T(8,128)(2,1)} %bitcast.7, s32[8,16]{1,0:T(8,128)S(1)} %bitcast.5, s32[2,128]{1,0:T(2,128)S(1)} %bitcast.6), custom_call_target="tpu_custom_call" | custom-call | tf_op jit(solution)/shard_map/pallas_call | solution.py:379
  103.5 0.7 copy.5
Async XLA Ops:
  0.0 0.7 copy-start
  0.7 0.7 copy-start.1

commit v6 on v5

--- a/solution.py
+++ b/solution.py
@@ -20,24 +20,24 @@
 CHUNKS = (
     ((0, 128, "S", 2, 0), (128, 128, "S", 2, 0), (0, 128, "S", 2, 1), (128, 128, "S", 2, 1),),
     ((0, 128, "S", 2, 0), (128, 128, "S", 2, 0), (0, 128, "S", 2, 1), (128, 128, "S", 2, 1),),
-    ((0, 128, "S", 2, 0), (128, 128, "Z", 2, 0), (0, 128, "Y", 2, 1), (128, 128, "Z", 2, 1),),
+    ((0, 128, "S", 2, 0), (128, 128, "S", 2, 0), (0, 128, "Y", 2, 1), (128, 128, "S", 2, 1),),
 )
 ORDER = (
-    ("m", 0, 0), ("F", 0, 0), ("n", 0, 0), ("F", 0, 1), ("N", 0, 0), ("o", 0, 0), ("m", 0, 1), ("N", 0, 1),
-    ("C", 0, 0), ("C", 0, 1), ("n", 0, 1), ("F", 0, 2), ("A", 0, 0), ("N", 0, 2), ("F", 0, 3), ("A", 0, 1),
-    ("N", 0, 3), ("E", 0, 0), ("C", 0, 2), ("E", 0, 1), ("o", 0, 1), ("C", 0, 3), ("P", 0, 0), ("A", 0, 2),
-    ("P", 0, 1), ("L", 0, 1), ("L", 0, 0), ("A", 0, 3), ("M", 0, 0), ("M", 0, 1), ("E", 0, 2), ("E", 0, 3),
+    ("m", 0, 0), ("F", 0, 0), ("n", 0, 0), ("N", 0, 0), ("F", 0, 1), ("C", 0, 0), ("m", 0, 1), ("o", 0, 0),
+    ("N", 0, 1), ("C", 0, 1), ("A", 0, 0), ("F", 0, 2), ("n", 0, 1), ("N", 0, 2), ("A", 0, 1), ("F", 0, 3),
+    ("E", 0, 0), ("C", 0, 2), ("o", 0, 1), ("N", 0, 3), ("E", 0, 1), ("C", 0, 3), ("P", 0, 0), ("A", 0, 2),
+    ("L", 0, 0), ("P", 0, 1), ("L", 0, 1), ("A", 0, 3), ("M", 0, 0), ("M", 0, 1), ("E", 0, 2), ("E", 0, 3),
     ("V", 0, 0), ("S", 0, 0), ("S", 0, 1), ("P", 0, 2), ("P", 0, 3), ("L", 0, 2), ("L", 0, 3), ("X", 0, 0),
-    ("U", 0, 0), ("m", 1, 0), ("F", 1, 0), ("M", 0, 2), ("n", 1, 0), ("F", 1, 1), ("M", 0, 3), ("N", 1, 0),
-    ("C", 1, 0), ("S", 0, 2), ("S", 0, 3), ("N", 1, 1), ("C", 1, 1), ("o", 1, 0), ("X", 0, 1), ("m", 1, 1),
-    ("F", 1, 2), ("A", 1, 0), ("F", 1, 3), ("n", 1, 1), ("N", 1, 3), ("A", 1, 1), ("N", 1, 2), ("E", 1, 0),
-    ("C", 1, 2), ("o", 1, 1), ("E", 1, 1), ("C", 1, 3), ("L", 1, 0), ("P", 1, 0), ("A", 1, 2), ("P", 1, 1),
-    ("A", 1, 3), ("L", 1, 1), ("M", 1, 0), ("E", 1, 2), ("M", 1, 1), ("E", 1, 3), ("V", 1, 0), ("P", 1, 2),
-    ("S", 1, 0), ("L", 1, 3), ("L", 1, 2), ("P", 1, 3), ("S", 1, 1), ("U", 1, 0), ("M", 1, 2), ("X", 1, 0),
-    ("M", 1, 3), ("m", 2, 0), ("F", 2, 0), ("n", 2, 0), ("S", 1, 2), ("N", 2, 0), ("S", 1, 3), ("o", 2, 0),
-    ("F", 2, 1), ("C", 2, 0), ("X", 1, 1), ("m", 2, 1), ("n", 2, 1), ("o", 2, 1), ("Y", 2, 2), ("F", 2, 3),
-    ("C", 2, 1), ("C", 2, 3), ("A", 2, 0), ("A", 2, 1), ("W", 2, 2), ("A", 2, 3), ("C", 2, 2), ("E", 2, 0),
-    ("E", 2, 1), ("E", 2, 3), ("E", 2, 2), ("V", 2, 0),
+    ("U", 0, 0), ("m", 1, 0), ("M", 0, 2), ("F", 1, 0), ("M", 0, 3), ("F", 1, 1), ("n", 1, 0), ("N", 1, 0),
+    ("S", 0, 2), ("C", 1, 0), ("S", 0, 3), ("C", 1, 1), ("N", 1, 1), ("o", 1, 0), ("X", 0, 1), ("m", 1, 1),
+    ("A", 1, 0), ("F", 1, 2), ("n", 1, 1), ("N", 1, 2), ("A", 1, 1), ("F", 1, 3), ("E", 1, 0), ("C", 1, 2),
+    ("o", 1, 1), ("N", 1, 3), ("E", 1, 1), ("C", 1, 3), ("P", 1, 0), ("A", 1, 2), ("L", 1, 0), ("P", 1, 1),
+    ("A", 1, 3), ("M", 1, 0), ("L", 1, 1), ("E", 1, 2), ("M", 1, 1), ("E", 1, 3), ("V", 1, 0), ("P", 1, 2),
+    ("S", 1, 0), ("L", 1, 2), ("P", 1, 3), ("S", 1, 1), ("M", 1, 2), ("U", 1, 0), ("X", 1, 0), ("L", 1, 3),
+    ("M", 1, 3), ("m", 2, 0), ("n", 2, 0), ("S", 1, 2), ("F", 2, 1), ("N", 2, 1), ("S", 1, 3), ("o", 2, 0),
+    ("F", 2, 0), ("N", 2, 0), ("X", 1, 1), ("m", 2, 1), ("n", 2, 1), ("o", 2, 1), ("Y", 2, 2), ("F", 2, 3),
+    ("C", 2, 1), ("C", 2, 0), ("C", 2, 3), ("N", 2, 3), ("A", 2, 1), ("A", 2, 0), ("W", 2, 2), ("A", 2, 3),
+    ("E", 2, 1), ("C", 2, 2), ("E", 2, 0), ("E", 2, 3), ("E", 2, 2), ("V", 2, 0),
 )
 NQ = len(CHUNKS[0])
 HALF = C // 2

time: 104 us -> 103 us (level)
  Pallas kernels: 102 us -> 100 us
    pallas_call x1, Pallas kernels: 102 us -> 100 us  [on_device(): pl.pallas_call(kernel, out_shape=jax.ShapeDtypeStruct((ROWS, C), BF16), i...]
where the time goes in v6:
time: 103 us; the launch traced here: 102 us
  Pallas kernels  100 us (97%)
  local copies, waits for them, and re-layouts  2.07 us (2%)
    pallas_call x1, Pallas kernels, on_device(): pl.pallas_call(kernel, out_shape=jax.ShapeDtypeStruct((ROWS, C), BF16), i...  100 us
    unnamed x5, local copies, waits for them, and re-layouts  2.07 us

profile of v6, /device:TPU:0, one launch (start us, length us, event | category | flops | bytes accessed | tf_op | source)
XLA Modules:
  0.0 102.4 jit_solution(7711567332076401933)
XLA Ops:
  0.0 0.0 copy-start
  0.0 0.7 copy-done
  0.7 0.0 copy-start.1
  0.7 0.7 copy-done.1
  1.4 100.4 %shard_map.37 = bf16[256,512]{1,0:T(8,128)(2,1)S(1)} custom-call(bf16[16,8,128,128]{3,2,1,0:T(8,128)(2,1)} %bitcast.7, s32[8,16]{1,0:T(8,128)S(1)} %bitcast.5, s32[2,128]{1,0:T(2,128)S(1)} %bitcast.6), custom_call_target="tpu_custom_call" | custom-call | tf_op jit(solution)/shard_map/pallas_call | solution.py:379
  101.7 0.7 copy.5
Async XLA Ops:
  0.0 0.7 copy-start
  0.7 0.7 copy-start.1

commit v7 on v6

--- a/solution.py
+++ b/solution.py
@@ -18,26 +18,27 @@
 BF16 = jnp.bfloat16
 
 CHUNKS = (
-    ((0, 128, "S", 2, 0), (128, 128, "S", 2, 0), (0, 128, "S", 2, 1), (128, 128, "S", 2, 1),),
-    ((0, 128, "S", 2, 0), (128, 128, "S", 2, 0), (0, 128, "S", 2, 1), (128, 128, "S", 2, 1),),
+    ((0, 128, "S", 4, 0), (128, 128, "S", 4, 0), (0, 128, "S", 2, 1), (128, 128, "S", 2, 1),),
+    ((0, 128, "S", 4, 0), (128, 128, "S", 4, 0), (0, 128, "S", 2, 1), (128, 128, "S", 2, 1),),
     ((0, 128, "S", 2, 0), (128, 128, "S", 2, 0), (0, 128, "Y", 2, 1), (128, 128, "S", 2, 1),),
 )
 ORDER = (
-    ("m", 0, 0), ("F", 0, 0), ("n", 0, 0), ("N", 0, 0), ("F", 0, 1), ("C", 0, 0), ("m", 0, 1), ("o", 0, 0),
-    ("N", 0, 1), ("C", 0, 1), ("A", 0, 0), ("F", 0, 2), ("n", 0, 1), ("N", 0, 2), ("A", 0, 1), ("F", 0, 3),
-    ("E", 0, 0), ("C", 0, 2), ("o", 0, 1), ("N", 0, 3), ("E", 0, 1), ("C", 0, 3), ("P", 0, 0), ("A", 0, 2),
-    ("L", 0, 0), ("P", 0, 1), ("L", 0, 1), ("A", 0, 3), ("M", 0, 0), ("M", 0, 1), ("E", 0, 2), ("E", 0, 3),
-    ("V", 0, 0), ("S", 0, 0), ("S", 0, 1), ("P", 0, 2), ("P", 0, 3), ("L", 0, 2), ("L", 0, 3), ("X", 0, 0),
-    ("U", 0, 0), ("m", 1, 0), ("M", 0, 2), ("F", 1, 0), ("M", 0, 3), ("F", 1, 1), ("n", 1, 0), ("N", 1, 0),
-    ("S", 0, 2), ("C", 1, 0), ("S", 0, 3), ("C", 1, 1), ("N", 1, 1), ("o", 1, 0), ("X", 0, 1), ("m", 1, 1),
-    ("A", 1, 0), ("F", 1, 2), ("n", 1, 1), ("N", 1, 2), ("A", 1, 1), ("F", 1, 3), ("E", 1, 0), ("C", 1, 2),
-    ("o", 1, 1), ("N", 1, 3), ("E", 1, 1), ("C", 1, 3), ("P", 1, 0), ("A", 1, 2), ("L", 1, 0), ("P", 1, 1),
-    ("A", 1, 3), ("M", 1, 0), ("L", 1, 1), ("E", 1, 2), ("M", 1, 1), ("E", 1, 3), ("V", 1, 0), ("P", 1, 2),
-    ("S", 1, 0), ("L", 1, 2), ("P", 1, 3), ("S", 1, 1), ("M", 1, 2), ("U", 1, 0), ("X", 1, 0), ("L", 1, 3),
-    ("M", 1, 3), ("m", 2, 0), ("n", 2, 0), ("S", 1, 2), ("F", 2, 1), ("N", 2, 1), ("S", 1, 3), ("o", 2, 0),
-    ("F", 2, 0), ("N", 2, 0), ("X", 1, 1), ("m", 2, 1), ("n", 2, 1), ("o", 2, 1), ("Y", 2, 2), ("F", 2, 3),
+    ("m", 0, 0), ("F", 0, 0), ("n", 0, 0), ("F", 0, 1), ("m", 0, 1), ("o", 0, 0), ("N", 0, 0), ("C", 0, 0),
+    ("n", 0, 1), ("C", 0, 1), ("N", 0, 1), ("A", 0, 0), ("F", 0, 2), ("o", 0, 1), ("F", 0, 3), ("A", 0, 1),
+    ("N", 0, 2), ("E", 0, 0), ("N", 0, 3), ("C", 0, 2), ("E", 0, 1), ("L", 0, 0), ("C", 0, 3), ("P", 0, 0),
+    ("A", 0, 2), ("P", 0, 1), ("A", 0, 3), ("L", 0, 1), ("M", 0, 0), ("K", 0, 0), ("M", 0, 1), ("E", 0, 2),
+    ("E", 0, 3), ("V", 0, 0), ("S", 0, 0), ("K", 0, 1), ("R", 0, 0), ("R", 0, 1), ("S", 0, 1), ("L", 0, 2),
+    ("P", 0, 2), ("L", 0, 3), ("X", 0, 0), ("P", 0, 3), ("U", 0, 0), ("m", 1, 0), ("F", 1, 0), ("M", 0, 2),
+    ("M", 0, 3), ("F", 1, 1), ("n", 1, 0), ("N", 1, 0), ("C", 1, 0), ("S", 0, 2), ("S", 0, 3), ("C", 1, 1),
+    ("N", 1, 1), ("o", 1, 0), ("X", 0, 1), ("m", 1, 1), ("A", 1, 0), ("F", 1, 2), ("n", 1, 1), ("N", 1, 2),
+    ("A", 1, 1), ("F", 1, 3), ("E", 1, 0), ("C", 1, 2), ("o", 1, 1), ("N", 1, 3), ("E", 1, 1), ("C", 1, 3),
+    ("P", 1, 0), ("L", 1, 0), ("A", 1, 2), ("L", 1, 1), ("P", 1, 1), ("A", 1, 3), ("M", 1, 0), ("E", 1, 2),
+    ("K", 1, 0), ("M", 1, 1), ("E", 1, 3), ("R", 1, 0), ("V", 1, 0), ("P", 1, 2), ("K", 1, 1), ("L", 1, 2),
+    ("S", 1, 0), ("R", 1, 1), ("S", 1, 1), ("P", 1, 3), ("X", 1, 0), ("M", 1, 2), ("L", 1, 3), ("U", 1, 0),
+    ("M", 1, 3), ("m", 2, 0), ("n", 2, 0), ("S", 1, 2), ("F", 2, 1), ("S", 1, 3), ("F", 2, 0), ("N", 2, 0),
+    ("N", 2, 1), ("o", 2, 0), ("X", 1, 1), ("m", 2, 1), ("n", 2, 1), ("o", 2, 1), ("Y", 2, 2), ("F", 2, 3),
     ("C", 2, 1), ("C", 2, 0), ("C", 2, 3), ("N", 2, 3), ("A", 2, 1), ("A", 2, 0), ("W", 2, 2), ("A", 2, 3),
-    ("E", 2, 1), ("C", 2, 2), ("E", 2, 0), ("E", 2, 3), ("E", 2, 2), ("V", 2, 0),
+    ("C", 2, 2), ("E", 2, 0), ("E", 2, 1), ("E", 2, 3), ("E", 2, 2), ("V", 2, 0),
 )
 NQ = len(CHUNKS[0])
 HALF = C // 2

time: 103 us -> 102 us (level)
  no operation moved by 1% of the time
where the time goes in v7:
time: 102 us
  Pallas kernels  99.6 us (98%)
  local copies, waits for them, and re-layouts  2.07 us (2%)
    pallas_call x1, Pallas kernels, on_device(): pl.pallas_call(kernel, out_shape=jax.ShapeDtypeStruct((ROWS, C), BF16), i...  99.6 us
    unnamed x5, local copies, waits for them, and re-layouts  2.07 us

profile of v7, /device:TPU:0, one launch (start us, length us, event | category | flops | bytes accessed | tf_op | source)
XLA Modules:
  0.0 101.7 jit_solution(11851640938464656688)
XLA Ops:
  0.0 0.0 copy-start
  0.0 0.7 copy-done
  0.7 0.0 copy-start.1
  0.7 0.7 copy-done.1
  1.4 99.6 %shard_map.37 = bf16[256,512]{1,0:T(8,128)(2,1)S(1)} custom-call(bf16[16,8,128,128]{3,2,1,0:T(8,128)(2,1)} %bitcast.7, s32[8,16]{1,0:T(8,128)S(1)} %bitcast.5, s32[2,128]{1,0:T(2,128)S(1)} %bitcast.6), custom_call_target="tpu_custom_call" | custom-call | tf_op jit(solution)/shard_map/pallas_call | solution.py:380
  101.0 0.7 copy.5
Async XLA Ops:
  0.0 0.7 copy-start
  0.7 0.7 copy-start.1

commit v8 on v7

--- a/solution.py
+++ b/solution.py
@@ -20,25 +20,25 @@
 CHUNKS = (
     ((0, 128, "S", 4, 0), (128, 128, "S", 4, 0), (0, 128, "S", 2, 1), (128, 128, "S", 2, 1),),
     ((0, 128, "S", 4, 0), (128, 128, "S", 4, 0), (0, 128, "S", 2, 1), (128, 128, "S", 2, 1),),
-    ((0, 128, "S", 2, 0), (128, 128, "S", 2, 0), (0, 128, "Y", 2, 1), (128, 128, "S", 2, 1),),
+    ((0, 128, "S", 2, 0), (128, 128, "Z", 2, 0), (0, 128, "Y", 2, 1), (128, 128, "Z", 2, 1),),
 )
 ORDER = (
-    ("m", 0, 0), ("F", 0, 0), ("n", 0, 0), ("F", 0, 1), ("m", 0, 1), ("o", 0, 0), ("N", 0, 0), ("C", 0, 0),
-    ("n", 0, 1), ("C", 0, 1), ("N", 0, 1), ("A", 0, 0), ("F", 0, 2), ("o", 0, 1), ("F", 0, 3), ("A", 0, 1),
-    ("N", 0, 2), ("E", 0, 0), ("N", 0, 3), ("C", 0, 2), ("E", 0, 1), ("L", 0, 0), ("C", 0, 3), ("P", 0, 0),
-    ("A", 0, 2), ("P", 0, 1), ("A", 0, 3), ("L", 0, 1), ("M", 0, 0), ("K", 0, 0), ("M", 0, 1), ("E", 0, 2),
-    ("E", 0, 3), ("V", 0, 0), ("S", 0, 0), ("K", 0, 1), ("R", 0, 0), ("R", 0, 1), ("S", 0, 1), ("L", 0, 2),
-    ("P", 0, 2), ("L", 0, 3), ("X", 0, 0), ("P", 0, 3), ("U", 0, 0), ("m", 1, 0), ("F", 1, 0), ("M", 0, 2),
+    ("m", 0, 0), ("F", 0, 0), ("n", 0, 0), ("N", 0, 0), ("F", 0, 1), ("m", 0, 1), ("C", 0, 0), ("N", 0, 1),
+    ("o", 0, 0), ("C", 0, 1), ("n", 0, 1), ("F", 0, 2), ("A", 0, 0), ("F", 0, 3), ("N", 0, 2), ("A", 0, 1),
+    ("N", 0, 3), ("E", 0, 0), ("C", 0, 2), ("E", 0, 1), ("o", 0, 1), ("C", 0, 3), ("P", 0, 0), ("A", 0, 2),
+    ("P", 0, 1), ("A", 0, 3), ("L", 0, 0), ("M", 0, 0), ("L", 0, 1), ("K", 0, 0), ("M", 0, 1), ("E", 0, 2),
+    ("R", 0, 1), ("E", 0, 3), ("V", 0, 0), ("K", 0, 1), ("S", 0, 0), ("R", 0, 0), ("S", 0, 1), ("P", 0, 2),
+    ("X", 0, 0), ("P", 0, 3), ("L", 0, 2), ("L", 0, 3), ("U", 0, 0), ("m", 1, 0), ("F", 1, 0), ("M", 0, 2),
     ("M", 0, 3), ("F", 1, 1), ("n", 1, 0), ("N", 1, 0), ("C", 1, 0), ("S", 0, 2), ("S", 0, 3), ("C", 1, 1),
-    ("N", 1, 1), ("o", 1, 0), ("X", 0, 1), ("m", 1, 1), ("A", 1, 0), ("F", 1, 2), ("n", 1, 1), ("N", 1, 2),
+    ("o", 1, 0), ("N", 1, 1), ("X", 0, 1), ("m", 1, 1), ("A", 1, 0), ("F", 1, 2), ("n", 1, 1), ("N", 1, 2),
     ("A", 1, 1), ("F", 1, 3), ("E", 1, 0), ("C", 1, 2), ("o", 1, 1), ("N", 1, 3), ("E", 1, 1), ("C", 1, 3),
-    ("P", 1, 0), ("L", 1, 0), ("A", 1, 2), ("L", 1, 1), ("P", 1, 1), ("A", 1, 3), ("M", 1, 0), ("E", 1, 2),
-    ("K", 1, 0), ("M", 1, 1), ("E", 1, 3), ("R", 1, 0), ("V", 1, 0), ("P", 1, 2), ("K", 1, 1), ("L", 1, 2),
-    ("S", 1, 0), ("R", 1, 1), ("S", 1, 1), ("P", 1, 3), ("X", 1, 0), ("M", 1, 2), ("L", 1, 3), ("U", 1, 0),
-    ("M", 1, 3), ("m", 2, 0), ("n", 2, 0), ("S", 1, 2), ("F", 2, 1), ("S", 1, 3), ("F", 2, 0), ("N", 2, 0),
-    ("N", 2, 1), ("o", 2, 0), ("X", 1, 1), ("m", 2, 1), ("n", 2, 1), ("o", 2, 1), ("Y", 2, 2), ("F", 2, 3),
-    ("C", 2, 1), ("C", 2, 0), ("C", 2, 3), ("N", 2, 3), ("A", 2, 1), ("A", 2, 0), ("W", 2, 2), ("A", 2, 3),
-    ("C", 2, 2), ("E", 2, 0), ("E", 2, 1), ("E", 2, 3), ("E", 2, 2), ("V", 2, 0),
+    ("P", 1, 0), ("L", 1, 0), ("A", 1, 2), ("P", 1, 1), ("A", 1, 3), ("M", 1, 0), ("L", 1, 1), ("K", 1, 0),
+    ("E", 1, 2), ("R", 1, 0), ("M", 1, 1), ("E", 1, 3), ("R", 1, 1), ("V", 1, 0), ("P", 1, 2), ("K", 1, 1),
+    ("S", 1, 0), ("L", 1, 2), ("S", 1, 1), ("P", 1, 3), ("L", 1, 3), ("X", 1, 0), ("M", 1, 2), ("U", 1, 0),
+    ("m", 2, 0), ("M", 1, 3), ("F", 2, 0), ("n", 2, 0), ("N", 2, 0), ("S", 1, 2), ("S", 1, 3), ("F", 2, 1),
+    ("C", 2, 0), ("o", 2, 0), ("X", 1, 1), ("m", 2, 1), ("n", 2, 1), ("o", 2, 1), ("Y", 2, 2), ("F", 2, 3),
+    ("C", 2, 1), ("C", 2, 3), ("A", 2, 1), ("A", 2, 0), ("W", 2, 2), ("A", 2, 3), ("C", 2, 2), ("E", 2, 0),
+    ("E", 2, 3), ("E", 2, 1), ("E", 2, 2), ("V", 2, 0),
 )
 NQ = len(CHUNKS[0])
 HALF = C // 2
@@ -89,6 +89,16 @@
         )
     for other in (above, below, beside):
         pl.semaphore_signal(barrier, inc=1, device_id={"team": other, "rep": r}, device_id_type=MESH)
+    channel = lax.broadcasted_iota(jnp.int32, (BLK, HALF), 1)
+
+    def seed(at, rows_of):
+        for h in range(2):
+            label = rows_of(h)[:, None]
+            for n in range(2):
+                x0 = xs[0][n]
+                x0[at // 2, at % 2, h] = jnp.where(label == channel + n * HALF, 16.0, 0.0).astype(BF16)
+
+    seed(0, lambda h: lab[h])
     pl.semaphore_wait(barrier, N_REP - 1 + 3)
 
     lab_copies = []
@@ -98,16 +108,6 @@
             remote(lab, lab_all.at[at], lab_send, lab_recv.at[k], rep=rep_of(dx, dyh, dc))
         )
         lab_copies[-1].start()
-    channel = lax.broadcasted_iota(jnp.int32, (BLK, HALF), 1)
-
-    def seed(at, rows_of):
-        for h in range(2):
-            label = rows_of(h)[:, None]
-            for n in range(2):
-                x0 = xs[0][n]
-                x0[at // 2, at % 2, h] = jnp.where(label == channel + n * HALF, 16.0, 0.0).astype(BF16)
-
-    seed(0, lambda h: lab[h])
     for k in reversed(range(N_REP - 1)):
         dc, dx, dyh = others[k]
         at = dc * 8 + (4 - dx) % 4 * 2 + dyh

time: 102 us -> 102 us (level)
  no operation moved by 1% of the time
where the time goes in v8:
time: 102 us
  Pallas kernels  99.8 us (98%)
  local copies, waits for them, and re-layouts  2.07 us (2%)
    pallas_call x1, Pallas kernels, on_device(): pl.pallas_call(kernel, out_shape=jax.ShapeDtypeStruct((ROWS, C), BF16), i...  99.8 us
    unnamed x5, local copies, waits for them, and re-layouts  2.07 us

profile of v8, /device:TPU:0, one launch (start us, length us, event | category | flops | bytes accessed | tf_op | source)
XLA Modules:
  0.0 101.9 jit_solution(10671239088086576536)
XLA Ops:
  0.0 0.0 copy-start
  0.0 0.7 copy-done
  0.7 0.0 copy-start.1
  0.7 0.7 copy-done.1
  1.4 99.8 %shard_map.37 = bf16[256,512]{1,0:T(8,128)(2,1)S(1)} custom-call(bf16[16,8,128,128]{3,2,1,0:T(8,128)(2,1)} %bitcast.7, s32[8,16]{1,0:T(8,128)S(1)} %bitcast.5, s32[2,128]{1,0:T(2,128)S(1)} %bitcast.6), custom_call_target="tpu_custom_call" | custom-call | tf_op jit(solution)/shard_map/pallas_call | solution.py:380
  101.2 0.7 copy.5
Async XLA Ops:
  0.0 0.7 copy-start
  0.7 0.7 copy-start.1
